TPU v7x, 128 devices: a whole 4x4x4 slice. The times are simulated.
128 devices in a mesh: leaf: 32 (over z, y, core), sub: 4 (over x).
Axes of the slice: x: 4, y: 4, z: 4, core: 2. Of those that a mesh axis runs over, the one named last changes fastest.
Arguments:
- density: float32 [4, 2048, 128], P(None, ('leaf', 'sub')), may hold values from -6 to 6
- centres: float32 [3, 2048, 128], P(None, ('leaf', 'sub')), may hold values from 0 to 1
- normal: float32 [3, 2048, 128], P(None, ('leaf', 'sub')), may hold values from -0.10206208 to 0.10206208
- to_multipole: bfloat16 [2048, 152, 128], P(('leaf', 'sub')), may hold values from -0.5 to 0.5
- to_panels: bfloat16 [2048, 128, 152], P(('leaf', 'sub')), may hold values from -0.5 to 0.5
- m2m_ops: bfloat16 [8, 152, 152], replicated, may hold values from -0.5 to 0.5
- l2l_ops: bfloat16 [8, 152, 152], replicated, may hold values from -0.5 to 0.5
- m2l_ops: bfloat16 [316, 152, 152], replicated, may hold values from -0.078125 to 0.078125
- near_index: int32 [2048, 27], P(('leaf', 'sub')), may hold values from 0 to 23
- near_count: int32 [2048], P(('leaf', 'sub')), may hold values from 1 to 27
- send_box: int32 [128, 128, 2], P(('leaf', 'sub')), may hold values from 0 to 15
- send_count: int32 [128, 128], P(('leaf', 'sub')), may hold values from 0 to 2, as said below
- far_slot: int32 [2048, 64], P(('leaf', 'sub')), may hold values from 0 to 255, as said below
- far_op: int32 [2048, 64], P(('leaf', 'sub')), may hold values from 0 to 315
- far_count: int32 [2048], P(('leaf', 'sub')), may hold values from 1 to 64
- parent_of: int32 [32, 64], P('leaf', 'sub'), may hold values from 0 to 15, never falling along the last dimension, each value on 1 to 8 neighbouring positions
- octant: int32 [32, 64], P('leaf', 'sub'), may hold values from 0 to 7
- top_src: int32 [512, 32], P('leaf'), may hold values from 0 to 511
- top_op: int32 [512, 32], P('leaf'), may hold values from 0 to 315
- top_count: int32 [512], P('leaf'), may hold values from 1 to 32
Outputs:
- potential: float32 [4, 2048, 128], P(None, ('leaf', 'sub'))
Inputs may be any that keep to these rules, and one draw needn't show every extreme that they name: `parent_of`: within each row, parent numbers never fall, each of 0 to 15 appears, at most 8 times, one exactly 8 times. `send_count`: every device receives at least one valid slot; in every draw one receiving device gets 2 valid slots from every sender. `far_slot`: each entry of a leaf on device d is s * 2 + j with j < send_count[s, d].
All inputs are finite; a program needn't handle non-finite values.
Results may differ from a plain program's by a relative error of at most 0.002.
Values may be sent and summed in bfloat16 or wider, within the bound.
No kernel may reach another device: no remote copies, remote signals or barrier semaphores. Data moves between devices by JAX's collectives and lax.ppermute only.
A program may use at most 128 MiB of HBM per device.

v0:
```python
import jax
import jax.numpy as jnp
from jax import lax
from jax.experimental import pallas as pl
from jax.experimental.pallas import tpu as pltpu
from jax.sharding import PartitionSpec as P

f32 = jnp.float32
bf16 = jnp.bfloat16
i32 = jnp.int32

RIM = 4
LEAF = 16
RHS = 4
ROWS = RHS * LEAF
EQ = 152
EQP = 160
OPSP = 384
PAN = 128
BOX = 640
SLOT = 8
EPS = 0.01
FB = 8
MIB = 1 << 20

VM = pl.BlockSpec(memory_space=pltpu.VMEM)
SM = pl.BlockSpec(memory_space=pltpu.SMEM)


def nt(a, b, **kw):
    return lax.dot_general(a, b, (((1,), (1,)), ((), ())), preferred_element_type=f32, **kw)


def nn(a, b, **kw):
    return lax.dot_general(a, b, (((1,), (0,)), ((), ())), preferred_element_type=f32, **kw)


def iota(shape, dim):
    return lax.broadcasted_iota(i32, shape, dim)


def upward_kernel(par, octs, dens, cen, nrm, tm, m2m, mult_out, part_out, low_out, high_out):
    d = dens[...].astype(bf16)
    leaf_row = iota((ROWS, EQ), 0) % LEAF
    mult = jnp.zeros((ROWS, EQ), f32)
    for n in range(LEAF):
        mult = jnp.where(leaf_row == n, nt(d, tm[n]), mult)
    mb = mult.astype(bf16)
    mult_out[...] = mb
    child = jnp.zeros((ROWS, EQ), f32)
    for n in range(LEAF):
        child = jnp.where(leaf_row == n, nt(mb, m2m[octs[0, n]]), child)
    row = iota((ROWS, ROWS), 0)
    lane = iota((ROWS, ROWS), 1)
    parent = jnp.zeros((ROWS, ROWS), i32)
    for n in range(LEAF):
        parent = jnp.where(lane % LEAF == n, par[0, n], parent)
    box = (row // 16) * 4 + row % 4
    hit = (parent == box) & ((row // 4) % 4 == lane // LEAF)
    part_out[...] = nn(hit.astype(f32), child, precision=lax.Precision.HIGHEST)
    for a in range(3):
        high_out[4 * a : 4 * a + 4, :] = cen[a, :RIM, :]
        low_out[4 * a : 4 * a + 4, :] = cen[a, LEAF - RIM :, :]
        high_out[12 + 4 * a : 16 + 4 * a, :] = nrm[a, :RIM, :]
        low_out[12 + 4 * a : 16 + 4 * a, :] = nrm[a, LEAF - RIM :, :]
    for r in range(RHS):
        high_out[24 + 4 * r : 28 + 4 * r, :] = dens[LEAF * r : LEAF * r + RIM, :]
        low_out[24 + 4 * r : 28 + 4 * r, :] = dens[LEAF * (r + 1) - RIM : LEAF * (r + 1), :]


def upward(par, octs, dens, cen, nrm, tm, m2m):
    return pl.pallas_call(
        upward_kernel,
        in_specs=[SM, SM, VM, VM, VM, VM, VM],
        out_specs=[VM] * 4,
        out_shape=[
            jax.ShapeDtypeStruct((ROWS, EQ), bf16),
            jax.ShapeDtypeStruct((ROWS, EQ), f32),
            jax.ShapeDtypeStruct((40, PAN), f32),
            jax.ShapeDtypeStruct((40, PAN), f32),
        ],
        compiler_params=pltpu.CompilerParams(vmem_limit_bytes=16 * MIB),
        name="upward",
    )(par, octs, dens, cen, nrm, tm, m2m)


def pack_kernel(ids, mult, pieces, out):
    row = iota((EQ, BOX), 0)
    lane = iota((EQ, BOX), 1)
    own = pieces[0:16, :]
    for s in range(1, 4):
        own = own + pieces[16 * s : 16 * s + 16, :]
    own = own.astype(bf16).astype(f32)
    mf = mult[...].astype(f32)
    table = jnp.zeros((24, BOX), f32)
    for r in range(RHS):
        both = jnp.concatenate(
            [mf[16 * r : 16 * r + 16], own[4 * r : 4 * r + 4], jnp.zeros((4, EQ), f32)], 0
        )
        place = (lane == row + EQ * r).astype(f32).astype(bf16)
        table = table + nn(both.astype(bf16), place)
    hot = (ids[...] == iota((128 * SLOT, 24), 1)).astype(f32).astype(bf16)
    out[...] = nn(hot, table.astype(bf16)).astype(bf16)


def pack(ids, mult, pieces):
    return pl.pallas_call(
        pack_kernel,
        in_specs=[VM] * 3,
        out_specs=VM,
        out_shape=jax.ShapeDtypeStruct((128 * SLOT, BOX), bf16),
        compiler_params=pltpu.CompilerParams(vmem_limit_bytes=24 * MIB),
        name="pack",
    )(ids, mult, pieces)


def reorder_kernel(src, out):
    e0 = pl.program_id(0) * 16
    ops = src.shape[2]
    row = iota((256, 256), 0)
    lane = iota((256, 256), 1)
    perm = (lane == (row % 16) * 16 + row // 16).astype(f32).astype(bf16)
    e_row = e0 + iota((16, 16, ops), 0)
    for j in range(10):
        block = src[:, 16 * j : 16 * j + 16, :]
        live = e_row < EQ
        if j == 9:
            live = live & (iota((16, 16, ops), 1) < EQ - 144)
        block = jnp.where(live, block, jnp.zeros((), bf16)).reshape(256, ops)
        moved = nn(perm, block).astype(bf16)
        moved = jnp.concatenate([moved, jnp.zeros((256, OPSP - ops), bf16)], 1)
        moved = moved.reshape(16, 16, OPSP)
        if j == 9:
            out[144:EQ] = moved[: EQ - 144]
        else:
            out[16 * j : 16 * j + 16] = moved


def reorder(tables):
    ops = tables.shape[2]
    return pl.pallas_call(
        reorder_kernel,
        grid=(10,),
        in_specs=[pl.BlockSpec((16, EQP, ops), lambda i: (i, 0, 0))],
        out_specs=pl.BlockSpec((EQ, 16, OPSP), lambda i: (0, i, 0)),
        out_shape=jax.ShapeDtypeStruct((EQ, EQP, OPSP), bf16),
        compiler_params=pltpu.CompilerParams(vmem_limit_bytes=32 * MIB),
        cost_estimate=pl.CostEstimate(
            flops=2 * 100 * 256 * 256 * 384, bytes_accessed=37_000_000, transcendentals=0
        ),
        name="reorder",
    )(tables)


SRC = LEAF + 2 * RIM
FEAT = 48
ORDERS = ((0, 0), (0, 1), (1, 0), (0, 2), (1, 1), (2, 0))


def three(x):
    a = x.astype(bf16).astype(f32)
    b = (x - a).astype(bf16).astype(f32)
    c = (x - a - b).astype(bf16).astype(f32)
    return a, b, c


def near_kernel(index, count, cen, nrm, dens, low, high, out, raw, fsrc, ftar, fs, dtab):
    for q in range(10):
        raw[q, 0:RIM, :] = low[4 * q : 4 * q + 4, :]
        raw[q, RIM + LEAF : SRC, :] = high[4 * q : 4 * q + 4, :]
        if q < 3:
            body = cen[q]
        elif q < 6:
            body = nrm[q - 3]
        else:
            body = dens[LEAF * (q - 6) : LEAF * (q - 5), :]
        raw[q, RIM : RIM + LEAF, :] = body
    xs = [raw[a] - 0.5 for a in range(3)]
    ns = [raw[3 + a] for a in range(3)]
    xt = [cen[a] - 0.5 for a in range(3)]
    xs3 = [three(v) for v in xs]
    ns3 = [three(v) for v in ns]
    xt3 = [three(v) for v in xt]
    ss = three(xs[0] * xs[0] + xs[1] * xs[1] + xs[2] * xs[2] + EPS)
    sn = three(xs[0] * ns[0] + xs[1] * ns[1] + xs[2] * ns[2])
    tt = three(xt[0] * xt[0] + xt[1] * xt[1] + xt[2] * xt[2])
    one_s = jnp.ones((SRC, PAN), f32)
    zero_s = jnp.zeros((SRC, PAN), f32)
    one = jnp.ones((LEAF, PAN), f32)
    zero = jnp.zeros((LEAF, PAN), f32)
    feats = []
    for a in range(3):
        for i, j in ORDERS:
            feats.append((xs3[a][i], -2.0 * xt3[a][j], zero))
            feats.append((ns3[a][i], zero, xt3[a][j]))
    for i in range(3):
        feats.append((ss[i], one, zero))
        feats.append((sn[i], zero, -one))
        feats.append((one_s, tt[i], zero))
    while len(feats) < FEAT:
        feats.append((zero_s, zero, zero))
    for k, (s, t1, t2) in enumerate(feats):
        fsrc[k * SRC : (k + 1) * SRC, :] = s
        ftar[0, k * LEAF : (k + 1) * LEAF, :] = t1
        ftar[1, k * LEAF : (k + 1) * LEAF, :] = t2
    for r in range(RHS):
        d = raw[6 + r]
        hi = d.astype(bf16).astype(f32)
        dtab[pl.ds(r, SRC, stride=8), :] = hi
        dtab[pl.ds(RHS + r, SRC, stride=8), :] = (d - hi).astype(bf16).astype(f32)

    def turn(m, carry):
        fs[m] = fsrc[pl.ds(m, FEAT, stride=SRC), :].T.astype(bf16)
        return carry

    lax.fori_loop(0, SRC, turn, 0)

    def weights(leaf, rhs):
        y = nn(fs[leaf], rhs)
        inv = lax.rsqrt(y[:, :PAN])
        k = y[:, PAN:] * (inv * inv * inv)
        hi = k.astype(bf16)
        lo = (k - hi.astype(f32)).astype(bf16)
        return jnp.concatenate([hi, lo], 1)

    def one_leaf(n, carry):
        rhs = jnp.concatenate(
            [ftar[0, pl.ds(n, FEAT, stride=LEAF), :], ftar[1, pl.ds(n, FEAT, stride=LEAF), :]], 1
        ).astype(bf16)
        total = count[n]

        def pair(i, acc):
            second = 2 * i + 1
            live = second < total
            m1 = index[n, 2 * i]
            m2 = jnp.where(live, index[n, jnp.minimum(second, index.shape[1] - 1)], m1)
            scale = jnp.where(live, 1.0, 0.0).astype(f32)
            both = jnp.concatenate([weights(m1, rhs), weights(m2, rhs)], 0)
            d1 = dtab[pl.ds(pl.multiple_of(m1 * 8, 8), 8), :]
            d2 = dtab[pl.ds(pl.multiple_of(m2 * 8, 8), 8), :] * scale
            d = jnp.concatenate([d1, d2], 1).astype(bf16)
            return acc + nn(d, both)

        acc = lax.fori_loop(0, (total + 1) // 2, pair, jnp.zeros((8, 2 * PAN), f32))
        acc = acc[:, :PAN] + acc[:, PAN:]
        out[pl.ds(n, RHS, stride=LEAF), :] = acc[:RHS] + acc[RHS:]
        return carry

    lax.fori_loop(0, LEAF, one_leaf, 0)


def near(index, count, cen, nrm, dens, low, high):
    return pl.pallas_call(
        near_kernel,
        in_specs=[SM, SM] + [VM] * 5,
        out_specs=VM,
        out_shape=jax.ShapeDtypeStruct((ROWS, PAN), f32),
        scratch_shapes=[
            pltpu.VMEM((10, SRC, PAN), f32),
            pltpu.VMEM((FEAT * SRC, PAN), f32),
            pltpu.VMEM((2, FEAT * LEAF, PAN), f32),
            pltpu.VMEM((SRC, PAN, FEAT), bf16),
            pltpu.VMEM((SRC * 8, PAN), f32),
        ],
        compiler_params=pltpu.CompilerParams(vmem_limit_bytes=24 * MIB),
        cost_estimate=pl.CostEstimate(
            flops=20_000_000_00, bytes_accessed=1_000_000, transcendentals=3_600_000
        ),
        name="near",
    )(index, count, cen, nrm, dens, low, high)


def finish_kernel(
    par, octs, slots, kinds, arrived, tables, l2l, tp, near_part, out, turned, picked, s0, s1, s2, acc
):
    step = pl.program_id(0)
    spread = (s0, s1, s2)
    groups = slots.shape[0]

    @pl.when(step == 0)
    def _():
        acc[...] = jnp.zeros_like(acc)
        for t in range(BOX // PAN):
            turned[PAN * t : PAN * (t + 1), :] = arrived[:, PAN * t : PAN * (t + 1)].T
        slot_row = iota((128 * SLOT, PAN), 0)

        def pick(g, carry):
            hot = (slot_row == slots[pl.ds(g, 1), :]).astype(f32).astype(bf16)
            picked[g] = nn(turned[: RHS * EQ, :], hot).astype(bf16)
            return carry

        lax.fori_loop(0, groups, pick, 0)

        def build(g, per, base):
            kind = jnp.broadcast_to(kinds[pl.ds(g, 1), :], (PAN, PAN)).T
            src = picked[g]
            for h in range(per):
                target = kind - h * OPSP
                hot = jnp.concatenate(
                    [
                        (target == iota((PAN, PAN), 1) + PAN * t).astype(f32).astype(bf16)
                        for t in range(3)
                    ],
                    1,
                )
                y = nn(src, hot)
                for r in range(RHS):
                    at = pl.multiple_of((base + r * LEAF + h) * EQ, 8)
                    for t in range(3):
                        spread[t][pl.ds(at, EQ), :] = y[
                            r * EQ : (r + 1) * EQ, PAN * t : PAN * (t + 1)
                        ]

        def far_group(g, carry):
            build(g, 2, g * 2)
            return carry

        def top_group(g, carry):
            build(g, 4, ROWS + (g - 8) * 4)
            return carry

        lax.fori_loop(0, 8, far_group, 0)
        lax.fori_loop(8, 12, top_group, 0)

    left = []
    right = []
    for i in range(FB):
        for t in range(3):
            left.append(spread[t][pl.ds(step * FB + i, 2 * ROWS, stride=EQ), :].astype(bf16))
        right.append(tables[i])
    acc[...] += nt(jnp.concatenate(left, 1), jnp.concatenate(right, 1))

    @pl.when(step == pl.num_programs(0) - 1)
    def _():
        far = acc[:ROWS, :EQ]
        top = acc[ROWS:, :EQ].astype(bf16)
        row = iota((ROWS, ROWS), 0)
        lane = iota((ROWS, ROWS), 1)
        parent = jnp.zeros((ROWS, ROWS), i32)
        for n in range(LEAF):
            parent = jnp.where(row % LEAF == n, par[0, n], parent)
        hit = (parent == lane % LEAF) & (row // LEAF == lane // LEAF)
        chosen = nn(hit.astype(f32).astype(bf16), top).astype(bf16)
        leaf_row = iota((ROWS, EQ), 0) % LEAF
        down = jnp.zeros((ROWS, EQ), f32)
        for n in range(LEAF):
            down = jnp.where(leaf_row == n, nt(chosen, l2l[octs[0, n]]), down)
        local = (down + far).astype(bf16)
        leaf_row = iota((ROWS, PAN), 0) % LEAF
        res = jnp.zeros((ROWS, PAN), f32)
        for n in range(LEAF):
            res = jnp.where(leaf_row == n, nn(local, tp[n]), res)
        out[...] = res + near_part[...]


def finish(par, octs, slots, kinds, arrived, tables, l2l, tp, near_part):
    def whole(x):
        return pl.BlockSpec(x.shape, lambda i: (0,) * x.ndim)

    sm = pl.BlockSpec(memory_space=pltpu.SMEM)
    return pl.pallas_call(
        finish_kernel,
        grid=(EQ // FB,),
        in_specs=[
            sm,
            sm,
            whole(slots),
            whole(kinds),
            whole(arrived),
            pl.BlockSpec((FB, EQP, OPSP), lambda i: (i, 0, 0)),
            whole(l2l),
            whole(tp),
            whole(near_part),
        ],
        out_specs=pl.BlockSpec((ROWS, PAN), lambda i: (0, 0)),
        out_shape=jax.ShapeDtypeStruct((ROWS, PAN), f32),
        scratch_shapes=[
            pltpu.VMEM((BOX, 128 * SLOT), bf16),
            pltpu.VMEM((12, RHS * EQ, PAN), bf16),
            pltpu.VMEM((2 * ROWS * EQ, PAN), f32),
            pltpu.VMEM((2 * ROWS * EQ, PAN), f32),
            pltpu.VMEM((2 * ROWS * EQ, PAN), f32),
            pltpu.VMEM((2 * ROWS, EQP), f32),
        ],
        compiler_params=pltpu.CompilerParams(vmem_limit_bytes=56 * MIB),
        name="finish",
    )(par, octs, slots, kinds, arrived, tables, l2l, tp, near_part)


def per_device(
    density,
    centres,
    normal,
    to_multipole,
    to_panels,
    m2m_ops,
    l2l_ops,
    m2l_ops,
    near_index,
    near_count,
    send_box,
    send_count,
    far_slot,
    far_op,
    far_count,
    parent_of,
    octant,
    top_src,
    top_op,
    top_count,
):
    dens = density.reshape(ROWS, PAN)
    mult, part, low, high = upward(parent_of, octant, dens, centres, normal, to_multipole, m2m_ops)

    axes = ("leaf", "sub")
    count = lax.axis_size("leaf") * lax.axis_size("sub")
    forward = [(i, i + 1) for i in range(count - 1)]
    backward = [(i + 1, i) for i in range(count - 1)]
    low = lax.ppermute(low, axes, forward)
    high = lax.ppermute(high, axes, backward)

    pieces = lax.all_to_all(part, "sub", split_axis=0, concat_axis=0, tiled=True)

    slot_id = jnp.arange(2, dtype=i32)[None, :]
    far_ids = jnp.where(slot_id < send_count[0][:, None], send_box[0], -1)
    own_ids = jnp.broadcast_to(
        jnp.array([16, 17, 18, 19, -1, -1], i32)[None, :], (count, SLOT - 2)
    )
    ids = jnp.concatenate([far_ids, own_ids], 1).reshape(count * SLOT, 1)
    outgoing = pack(ids, mult, pieces)
    arrived = lax.all_to_all(outgoing, axes, split_axis=0, concat_axis=0, tiled=True)

    tables = reorder(jnp.transpose(m2l_ops, (1, 2, 0)))
    near_part = near(near_index, near_count, centres, normal, dens, low, high)

    far_live = jnp.arange(far_slot.shape[1])[None, :] < far_count[:, None]
    far_rows = jnp.where(far_live, (far_slot // 2) * SLOT + far_slot % 2, -1)
    top_live = jnp.arange(top_src.shape[1])[None, :] < top_count[:, None]
    top_rows = jnp.where(top_live, (top_src // 4) * SLOT + 2 + top_src % 4, -1)
    slots = jnp.concatenate([far_rows.reshape(8, PAN), top_rows.reshape(4, PAN)], 0)
    far_kind = far_op + OPSP * (jnp.arange(LEAF, dtype=i32) % 2)[:, None]
    top_kind = top_op + OPSP * (jnp.arange(LEAF, dtype=i32) % 4)[:, None]
    kinds = jnp.concatenate([far_kind.reshape(8, PAN), top_kind.reshape(4, PAN)], 0)

    res = finish(
        parent_of,
        octant,
        slots,
        kinds,
        arrived,
        tables,
        l2l_ops,
        jnp.transpose(to_panels, (0, 2, 1)),
        near_part,
    )
    return res.reshape(RHS, LEAF, PAN)


def solution(mesh):
    both = ("leaf", "sub")
    return jax.shard_map(
        per_device,
        mesh=mesh,
        in_specs=(
            P(None, both, None),
            P(None, both, None),
            P(None, both, None),
            P(both, None, None),
            P(both, None, None),
            P(),
            P(),
            P(),
            P(both, None),
            P(both),
            P(both, None, None),
            P(both, None),
            P(both, None),
            P(both, None),
            P(both),
            P("leaf", "sub"),
            P("leaf", "sub"),
            P("leaf", None),
            P("leaf", None),
            P("leaf"),
        ),
        out_specs=P(None, both, None),
        check_vma=False,
    )
```

profile of v0, /device:TPU:101, one launch (start us, length us, event | category | flops | bytes accessed | tf_op | source)
XLA Modules:
  0.0 146.2 jit_solution(2912701299491132386)
XLA Ops:
  0.0 1.1 copy-done.1
  1.1 1.1 copy-done.2
  2.2 0.8 copy-done.4
  2.9 0.7 copy-done.6
  3.7 0.7 copy-done.8
  4.4 0.7 copy-done.10
  5.0 0.7 copy-done.11
  5.7 2.5 %upward.1 = (bf16[64,152]{1,0:T(8,128)(2,1)S(1)}, f32[64,152]{1,0:T(8,128)}, f32[40,128]{1,0:T(8,128)S(1)}, f32[40,128]{1,0:T(8,128)S(1)}) custom-call(s32[1,16]{1,0:T(1,128)S(1)} %copy-done.10, s32[1,16]{1,0:T(1,128)S(1)} %copy-done.11, f32[64,128]{1,0:T(8,128)S(1)} %bitcast.13, f32[3,16,128]{2,1,0:T(8,128)S(1)} %copy-done.6, f32[3,16,128]{2,1,0:T(8,128)S(1)} %copy-done.8, ...), custom_call_target="tpu_custom_call" | custom-call | tf_op jit(solution)/shard_map/upward/pallas_call | solution.py:72
  8.2 4.2 %all-to-all-start = ((f32[4,16,152]{2,1,0:T(8,128)}), f32[4,16,152]{2,1,0:T(8,128)S(1)}, u32[]{:S(2)}, u32[]{:S(2)}) async-start(f32[4,16,152]{2,1,0:T(8,128)} %bitcast.3), calls=%async_computation | async-start | bytes 131072 | tf_op jit(solution)/shard_map/all_to_all | solution.py:422
  12.4 2.8 %collective-permute-start = (f32[40,128]{1,0:T(8,128)S(1)}, f32[40,128]{1,0:T(8,128)S(1)}, u32[]{:S(2)}, u32[]{:S(2)}) collective-permute-start(f32[40,128]{1,0:T(8,128)S(1)} %get-tuple-element.11), channel_id=1, source_target_pairs={{0,1},{1,2},{2,3},{3,4},{4,5},{5,6},{6,7},{7,8},{8,9},{9,10},{10,1... | collective-permute-start | bytes 61448 | tf_op jit(solution)/shard_map/ppermute | solution.py:419
  15.2 2.5 %collective-permute-start.1 = (f32[40,128]{1,0:T(8,128)S(1)}, f32[40,128]{1,0:T(8,128)S(1)}, u32[]{:S(2)}, u32[]{:S(2)}) collective-permute-start(f32[40,128]{1,0:T(8,128)S(1)} %get-tuple-element.12), channel_id=1, source_target_pairs={{1,0},{2,1},{3,2},{4,3},{5,4},{6,5},{7,6},{8,7},{9,8},{10,9},{11,1... | collective-permute-start | bytes 61448 | tf_op jit(solution)/shard_map/ppermute | solution.py:420
  17.7 0.7 pad.1.clone
  18.4 0.7 compare_select_fusion
  19.1 0.1 pad_add_fusion.2
  19.2 0.8 broadcast_add_fusion.1
  20.0 0.1 copy.25
  20.1 0.2 reshape.58.ids
  20.3 1.8 %pack.1 = bf16[1024,640]{1,0:T(8,128)(2,1)} custom-call(s32[1024,1]{1,0:T(8,128)S(1)} %reshape.58.ids, bf16[64,152]{1,0:T(8,128)(2,1)S(1)} %get-tuple-element.9.mult, f32[64,152]{1,0:T(8,128)S(1)} %bitcast.12), custom_call_target="tpu_custom_call" | custom-call | tf_op jit(solution)/shard_map/pack/pallas_call | solution.py:107
  22.1 11.3 %all-to-all-start.1 = ((bf16[128,8,640]{2,1,0:T(8,128)(2,1)}), bf16[128,8,640]{2,1,0:T(8,128)(2,1)S(1)}, u32[]{:S(2)}, u32[]{:S(2)}) async-start(bf16[128,8,640]{2,1,0:T(8,128)(2,1)} %bitcast.5), calls=%async_computation.1 | async-start | bytes 2621440 | tf_op jit(solution)/shard_map/all_to_all | solution.py:431
  33.3 0.8 broadcast_add_fusion
  34.2 0.1 reshape.54
  34.3 0.8 fusion.2
  35.0 0.1 reshape.51
  35.1 0.8 fusion.6
  35.9 0.1 reshape.52
  36.0 6.0 %copy-done = bf16[316,152,152]{0,2,1:T(8,128)(2,1)S(1)} copy-done((bf16[316,152,152]{0,2,1:T(8,128)(2,1)S(1)}, bf16[316,152,152]{0,2,1:T(8,128)(2,1)}, u32[]{:S(2)}) %copy-start) | copy-done | bytes 14601752
  42.0 13.3 %reorder.1.tables = bf16[152,160,384]{2,1,0:T(8,128)(2,1)} custom-call(bf16[152,152,316]{2,1,0:T(8,128)(2,1)S(1)} %bitcast.11), custom_call_target="tpu_custom_call" | custom-call | flops 5033164800 | bytes 37000000 | tf_op jit(solution)/shard_map/reorder/pallas_call | solution.py:141
  55.3 0.6 pad_add_fusion
  55.9 55.8 %near.1.near_part = f32[64,128]{1,0:T(8,128)S(1)} custom-call(s32[16,27]{1,0:T(8,128)S(1)} %copy-done.12, s32[16]{0:T(128)S(1)} %copy-done.13, f32[3,16,128]{2,1,0:T(8,128)S(1)} %copy-done.7, f32[3,16,128]{2,1,0:T(8,128)S(1)} %copy-done.9, f32[64,128]{1,0:T(8,128)S(1)} %bitcast.14, f32[40,128]{1,0:T(8,128)S(1)} %collective-permute-done.low, ...), custom_call_target="tpu_custom_call" | custom-call | flops 2000000000 | bytes 1000000 | tf_op jit(solution)/shard_map/near/pallas_call | solution.py:253
  111.8 0.6 copy-done.3
  112.4 1.1 copy-done.14
  113.5 32.7 %finish.1 = f32[64,128]{1,0:T(8,128)} custom-call(s32[1,16]{1,0:T(1,128)} %par.3, s32[1,16]{1,0:T(1,128)} %octs.3, s32[12,128]{1,0:T(8,128)} %get-tuple-element.13.slots, s32[12,128]{1,0:T(8,128)} %get-tuple-element.14.kinds, bf16[1024,640]{1,0:T(8,128)(2,1)} %bitcast.15, bf16[152,160,384]{2,1,0:T(8,128)(2,1)} %reorder.1.tables, bf16[8,152,152]{2,1,0:T(8,128)(2,1)} %l2l.1, ...), custom_call_target="tpu_custom_call" | custom-call | tf_op jit(solution)/shard_map/finish/pallas_call | solution.py:361
  (27 shorter events, 0.1 us)
Async XLA Ops:
  0.0 1.1 copy-start.1
  1.1 1.1 copy-start.2
  2.2 0.8 copy-start.4
  2.9 0.7 copy-start.6
  3.6 0.7 copy-start.8
  4.4 0.7 copy-start.10
  5.0 0.7 copy-start.11
  8.2 12.1 %all-to-all-start = ((f32[4,16,152]{2,1,0:T(8,128)}), f32[4,16,152]{2,1,0:T(8,128)S(1)}, u32[]{:S(2)}, u32[]{:S(2)}) async-start(f32[4,16,152]{2,1,0:T(8,128)} %bitcast.3), calls=%async_computation | async-start | bytes 131072 | tf_op jit(solution)/shard_map/all_to_all | solution.py:422
  12.4 43.5 %collective-permute-start = (f32[40,128]{1,0:T(8,128)S(1)}, f32[40,128]{1,0:T(8,128)S(1)}, u32[]{:S(2)}, u32[]{:S(2)}) collective-permute-start(f32[40,128]{1,0:T(8,128)S(1)} %get-tuple-element.11), channel_id=1, source_target_pairs={{0,1},{1,2},{2,3},{3,4},{4,5},{5,6},{6,7},{7,8},{8,9},{9,10},{10,1... | collective-permute-start | bytes 61448 | tf_op jit(solution)/shard_map/ppermute | solution.py:419
  15.2 40.7 %collective-permute-start.1 = (f32[40,128]{1,0:T(8,128)S(1)}, f32[40,128]{1,0:T(8,128)S(1)}, u32[]{:S(2)}, u32[]{:S(2)}) collective-permute-start(f32[40,128]{1,0:T(8,128)S(1)} %get-tuple-element.12), channel_id=1, source_target_pairs={{1,0},{2,1},{3,2},{4,3},{5,4},{6,5},{7,6},{8,7},{9,8},{10,9},{11,1... | collective-permute-start | bytes 61448 | tf_op jit(solution)/shard_map/ppermute | solution.py:420
  22.1 90.3 %all-to-all-start.1 = ((bf16[128,8,640]{2,1,0:T(8,128)(2,1)}), bf16[128,8,640]{2,1,0:T(8,128)(2,1)S(1)}, u32[]{:S(2)}, u32[]{:S(2)}) async-start(bf16[128,8,640]{2,1,0:T(8,128)(2,1)} %bitcast.5), calls=%async_computation.1 | async-start | bytes 2621440 | tf_op jit(solution)/shard_map/all_to_all | solution.py:431
  36.0 6.0 %copy-start = (bf16[316,152,152]{0,2,1:T(8,128)(2,1)S(1)}, bf16[316,152,152]{0,2,1:T(8,128)(2,1)}, u32[]{:S(2)}) copy-start(bf16[316,152,152]{0,2,1:T(8,128)(2,1)} %param.28) | copy-start | bytes 43805188
  42.0 13.9 %copy-start.5 = (f32[4,16,128]{2,1,0:T(8,128)S(1)}, f32[4,16,128]{2,1,0:T(8,128)}, u32[]{:S(2)}) copy-start(f32[4,16,128]{2,1,0:T(8,128)} %param.21) | copy-start | bytes 98308
  42.0 13.9 %copy-start.7 = (f32[3,16,128]{2,1,0:T(8,128)S(1)}, f32[3,16,128]{2,1,0:T(8,128)}, u32[]{:S(2)}) copy-start(f32[3,16,128]{2,1,0:T(8,128)} %cen.3) | copy-start | bytes 73732
  42.0 13.9 %copy-start.9 = (f32[3,16,128]{2,1,0:T(8,128)S(1)}, f32[3,16,128]{2,1,0:T(8,128)}, u32[]{:S(2)}) copy-start(f32[3,16,128]{2,1,0:T(8,128)} %nrm.3) | copy-start | bytes 73732
  42.0 13.9 %copy-start.12 = (s32[16,27]{1,0:T(8,128)S(1)}, s32[16,27]{1,0:T(8,128)}, u32[]{:S(2)}) copy-start(s32[16,27]{1,0:T(8,128)} %index.1) | copy-start | bytes 5188
  42.0 13.9 %copy-start.13 = (s32[16]{0:T(128)S(1)}, s32[16]{0:T(128)}, u32[]{:S(2)}) copy-start(s32[16]{0:T(128)} %count.1) | copy-start | bytes 196
  111.8 0.6 copy-start.3
  112.4 1.1 copy-start.14
where the time goes:
time: 147 us; the launch traced here: 146 us
  Pallas kernels  106 us (72%)
  starting transfers between devices  20.8 us (14%)
  local copies, waits for them, and re-layouts  14.8 us (10%)
  other arithmetic  4.45 us (3%)
    pallas_call x1, Pallas kernels, near(): pl.pallas_call(near_kernel, in_specs=[SM, SM] + [VM] * 5, out_specs=VM, o...  55.8 us
    pallas_call x1, Pallas kernels, finish(): pl.pallas_call(finish_kernel, grid=(EQ // FB,), in_specs=[sm, sm, whole(s...  32.7 us
    unnamed x30, local copies, waits for them, and re-layouts  13.4 us
    pallas_call x1, Pallas kernels, reorder(): pl.pallas_call(reorder_kernel, grid=(10,), in_specs=[pl.BlockSpec((16, EQ...  13.3 us
    all_to_all x1, starting transfers between devices, per_device(): lax.all_to_all(outgoing, axes, split_axis=0, concat_axis=0, tiled=True)  11.3 us
    all_to_all x1, starting transfers between devices, per_device(): lax.all_to_all(part, 'sub', split_axis=0, concat_axis=0, tiled=True)  4.24 us
  transfers between devices with their start and end apart: 4, of which 0 were waited for; matrix products, arithmetic and copies ran while one was open for 4% of the time, Pallas kernels for 48%

commit v1 on v0

v1 whole, which is shorter than its diff:
```python
import jax
import jax.numpy as jnp
from jax import lax
from jax.experimental import pallas as pl
from jax.experimental.pallas import tpu as pltpu
from jax.sharding import PartitionSpec as P

f32 = jnp.float32
bf16 = jnp.bfloat16
i32 = jnp.int32

RIM = 4
LEAF = 16
RHS = 4
ROWS = RHS * LEAF
EQ = 152
OPSP = 384
PAN = 128
BOX = 640
SLOT = 8
EPS = 0.01
FB = 16
MIB = 1 << 20
BIG = 56 * MIB

SM = pl.BlockSpec(memory_space=pltpu.SMEM)


def nt(a, b, **kw):
    return lax.dot_general(a, b, (((1,), (1,)), ((), ())), preferred_element_type=f32, **kw)


def nn(a, b, **kw):
    return lax.dot_general(a, b, (((1,), (0,)), ((), ())), preferred_element_type=f32, **kw)


def whole(x):
    return pl.BlockSpec(x.shape, lambda i: (0,) * len(x.shape))


def iota(shape, dim):
    return lax.broadcasted_iota(i32, shape, dim)


def upward_kernel(par, octs, dens, cen, nrm, tm, m2m, mult_out, part_out, low_out, high_out):
    d = dens[...].astype(bf16)
    leaf_row = iota((ROWS, EQ), 0) % LEAF
    mult = jnp.zeros((ROWS, EQ), f32)
    for n in range(LEAF):
        mult = jnp.where(leaf_row == n, nt(d, tm[n]), mult)
    mb = mult.astype(bf16)
    mult_out[...] = mb
    child = jnp.zeros((ROWS, EQ), f32)
    for n in range(LEAF):
        child = jnp.where(leaf_row == n, nt(mb, m2m[octs[0, n]]), child)
    row = iota((ROWS, ROWS), 0)
    lane = iota((ROWS, ROWS), 1)
    parent = jnp.zeros((ROWS, ROWS), i32)
    for n in range(LEAF):
        parent = jnp.where(lane % LEAF == n, par[0, n], parent)
    box = (row // 16) * 4 + row % 4
    hit = (parent == box) & ((row // 4) % 4 == lane // LEAF)
    part_out[...] = nn(hit.astype(f32), child, precision=lax.Precision.HIGHEST)
    for a in range(3):
        high_out[4 * a : 4 * a + 4, :] = cen[a, :RIM, :]
        low_out[4 * a : 4 * a + 4, :] = cen[a, LEAF - RIM :, :]
        high_out[12 + 4 * a : 16 + 4 * a, :] = nrm[a, :RIM, :]
        low_out[12 + 4 * a : 16 + 4 * a, :] = nrm[a, LEAF - RIM :, :]
    for r in range(RHS):
        high_out[24 + 4 * r : 28 + 4 * r, :] = dens[LEAF * r : LEAF * r + RIM, :]
        low_out[24 + 4 * r : 28 + 4 * r, :] = dens[LEAF * (r + 1) - RIM : LEAF * (r + 1), :]


def upward(par, octs, dens, cen, nrm, tm, m2m):
    outs = [
        jax.ShapeDtypeStruct((ROWS, EQ), bf16),
        jax.ShapeDtypeStruct((ROWS, EQ), f32),
        jax.ShapeDtypeStruct((40, PAN), f32),
        jax.ShapeDtypeStruct((40, PAN), f32),
    ]
    return pl.pallas_call(
        upward_kernel,
        grid=(1,),
        in_specs=[SM, SM] + [whole(x) for x in (dens, cen, nrm, tm, m2m)],
        out_specs=[whole(x) for x in outs],
        out_shape=outs,
        compiler_params=pltpu.CompilerParams(vmem_limit_bytes=BIG),
        name="upward",
    )(par, octs, dens, cen, nrm, tm, m2m)


def pack_kernel(ids, mult, pieces, out):
    row = iota((EQ, BOX), 0)
    lane = iota((EQ, BOX), 1)
    own = pieces[0:16, :]
    for s in range(1, 4):
        own = own + pieces[16 * s : 16 * s + 16, :]
    own = own.astype(bf16).astype(f32)
    mf = mult[...].astype(f32)
    table = jnp.zeros((24, BOX), f32)
    for r in range(RHS):
        both = jnp.concatenate(
            [mf[16 * r : 16 * r + 16], own[4 * r : 4 * r + 4], jnp.zeros((4, EQ), f32)], 0
        )
        place = (lane == row + EQ * r).astype(f32).astype(bf16)
        table = table + nn(both.astype(bf16), place)
    hot = (ids[...] == iota((128 * SLOT, 24), 1)).astype(f32).astype(bf16)
    out[...] = nn(hot, table.astype(bf16)).astype(bf16)


def pack(ids, mult, pieces):
    outs = jax.ShapeDtypeStruct((128 * SLOT, BOX), bf16)
    return pl.pallas_call(
        pack_kernel,
        grid=(1,),
        in_specs=[whole(x) for x in (ids, mult, pieces)],
        out_specs=whole(outs),
        out_shape=outs,
        compiler_params=pltpu.CompilerParams(vmem_limit_bytes=BIG),
        name="pack",
    )(ids, mult, pieces)


SRC = LEAF + 2 * RIM
BATCH = 4
FEAT = 48
ORDERS = ((0, 0), (0, 1), (1, 0), (0, 2), (1, 1), (2, 0))


def three(x):
    a = x.astype(bf16).astype(f32)
    b = (x - a).astype(bf16).astype(f32)
    c = (x - a - b).astype(bf16).astype(f32)
    return a, b, c


def near_kernel(index, count, cen, nrm, dens, low, high, out, raw, fsrc, ftar, fs, dpar, dwide, ft, sums, dist):
    for q in range(10):
        raw[q, 0:RIM, :] = low[4 * q : 4 * q + 4, :]
        raw[q, RIM + LEAF : SRC, :] = high[4 * q : 4 * q + 4, :]
        if q < 3:
            body = cen[q]
        elif q < 6:
            body = nrm[q - 3]
        else:
            body = dens[LEAF * (q - 6) : LEAF * (q - 5), :]
        raw[q, RIM : RIM + LEAF, :] = body
    xs = [raw[a] - 0.5 for a in range(3)]
    ns = [raw[3 + a] for a in range(3)]
    xt = [cen[a] - 0.5 for a in range(3)]
    xs3 = [three(v) for v in xs]
    ns3 = [three(v) for v in ns]
    xt3 = [three(v) for v in xt]
    ss = three(xs[0] * xs[0] + xs[1] * xs[1] + xs[2] * xs[2] + EPS)
    sn = three(xs[0] * ns[0] + xs[1] * ns[1] + xs[2] * ns[2])
    tt = three(xt[0] * xt[0] + xt[1] * xt[1] + xt[2] * xt[2])
    one_s = jnp.ones((SRC, PAN), f32)
    zero_s = jnp.zeros((SRC, PAN), f32)
    one = jnp.ones((LEAF, PAN), f32)
    zero = jnp.zeros((LEAF, PAN), f32)
    feats = []
    for a in range(3):
        for i, j in ORDERS:
            feats.append((xs3[a][i], -2.0 * xt3[a][j], zero))
            feats.append((ns3[a][i], zero, xt3[a][j]))
    for i in range(3):
        feats.append((ss[i], one, zero))
        feats.append((sn[i], zero, -one))
        feats.append((one_s, tt[i], zero))
    while len(feats) < FEAT:
        feats.append((zero_s, zero, zero))
    for k, (s, t1, t2) in enumerate(feats):
        fsrc[k * SRC : (k + 1) * SRC, :] = s
        ftar[0, k * LEAF : (k + 1) * LEAF, :] = t1
        ftar[1, k * LEAF : (k + 1) * LEAF, :] = t2
    for m in range(SRC):
        fs[m] = fsrc[pl.ds(m, FEAT, stride=SRC), :].T.astype(bf16)
    dcols = iota((16, RHS * PAN), 1) // PAN
    pick_r = (iota((16, RHS * PAN), 0) // 3 == dcols).astype(f32).astype(bf16)
    for r in range(RHS):
        for j, part in enumerate(three(raw[6 + r])):
            dpar[pl.ds(3 * r + j, SRC, stride=16), :] = part
            dpar[pl.ds(12 + j, SRC, stride=16), :] = zero_s
    dpar[pl.ds(15, SRC, stride=16), :] = zero_s
    for m in range(SRC):
        wide = nn(dpar[16 * m : 16 * m + 16, :].T.astype(bf16), pick_r)
        for r in range(RHS):
            dwide[m, r] = wide[:, PAN * r : PAN * (r + 1)]
    dwide[SRC] = jnp.zeros((RHS, PAN, PAN), f32)
    for n in range(LEAF):
        ft[n] = jnp.concatenate(
            [ftar[0, pl.ds(n, FEAT, stride=LEAF), :], ftar[1, pl.ds(n, FEAT, stride=LEAF), :]], 1
        ).astype(bf16)
    sums[...] = jnp.zeros_like(sums)
    dist[:, :, :PAN] = jnp.ones((BATCH, 2 * PAN, PAN), f32)
    dist[:, :, PAN:] = jnp.zeros((BATCH, 2 * PAN, PAN), f32)
    pairs = 0
    for n in range(LEAF):
        pairs = pairs + (count[n] + 1) // 2
    steps = (pairs + BATCH - 1) // BATCH + 1

    def step(_, carry):
        n, i = carry[0], carry[1]
        old = carry[2:]
        for u in range(BATCH):
            n1, p1, q1 = old[3 * u], old[3 * u + 1], old[3 * u + 2]
            inv = lax.rsqrt(dist[u, :, :PAN])
            k = dist[u, :, PAN:] * (inv * inv * inv)
            for r in range(RHS):
                term = k[:PAN] * dwide[p1, r] + k[PAN:] * dwide[q1, r]
                sums[n1, r] += jnp.sum(term.reshape(PAN // 8, 8, PAN), 0)
        fresh = []
        for u in range(BATCH):
            at = jnp.minimum(n, LEAF - 1)
            first = 2 * i
            live1 = n < LEAF
            live2 = live1 & (first + 1 < count[at])
            p = index[at, first]
            q = index[at, jnp.minimum(first + 1, index.shape[1] - 1)]
            dist[u] = nn(jnp.concatenate([fs[p], fs[q]], 0), ft[at])
            fresh += [at, jnp.where(live1, p, SRC), jnp.where(live2, q, SRC)]
            more = live1 & (first + 2 < count[at])
            n = jnp.where(more, n, n + 1)
            i = jnp.where(more, i + 1, 0)
        return (n, i) + tuple(fresh)

    start = [jnp.int32(0), jnp.int32(0)] + [jnp.int32(0), jnp.int32(SRC), jnp.int32(SRC)] * BATCH
    lax.fori_loop(0, steps, step, tuple(start))
    for r in range(RHS):
        out[LEAF * r : LEAF * (r + 1), :] = jnp.sum(sums[:, r], 1)


def near(index, count, cen, nrm, dens, low, high):
    outs = jax.ShapeDtypeStruct((ROWS, PAN), f32)
    return pl.pallas_call(
        near_kernel,
        grid=(1,),
        in_specs=[SM, SM] + [whole(x) for x in (cen, nrm, dens, low, high)],
        out_specs=whole(outs),
        out_shape=outs,
        scratch_shapes=[
            pltpu.VMEM((10, SRC, PAN), f32),
            pltpu.VMEM((FEAT * SRC, PAN), f32),
            pltpu.VMEM((2, FEAT * LEAF, PAN), f32),
            pltpu.VMEM((SRC, PAN, FEAT), bf16),
            pltpu.VMEM((SRC * 16, PAN), f32),
            pltpu.VMEM((SRC + 1, RHS, PAN, PAN), f32),
            pltpu.VMEM((LEAF, FEAT, 2 * PAN), bf16),
            pltpu.VMEM((LEAF, RHS, 8, PAN), f32),
            pltpu.VMEM((BATCH, 2 * PAN, 2 * PAN), f32),
        ],
        compiler_params=pltpu.CompilerParams(vmem_limit_bytes=BIG),
        cost_estimate=pl.CostEstimate(
            flops=20_000_000_00, bytes_accessed=1_000_000, transcendentals=3_600_000
        ),
        name="near",
    )(index, count, cen, nrm, dens, low, high)


def finish_kernel(
    par, octs, slots, kinds, arrived, ops0, ops1, l2l, tp, near_part, out,
    turned, picked, s0, s1, s2, m0, m1, m2, m3, m4, m5, acc,
):
    step = pl.program_id(0)
    spread = (s0, s1, s2)
    even = (m0, m1, m2)
    odd = (m3, m4, m5)
    tail = ops0.shape[2] - 2 * PAN

    @pl.when(step == 0)
    def _():
        acc[...] = jnp.zeros_like(acc)
        m2[...] = jnp.zeros_like(m2)
        m5[...] = jnp.zeros_like(m5)
        for t in range(BOX // PAN):
            turned[PAN * t : PAN * (t + 1), :] = arrived[:, PAN * t : PAN * (t + 1)].T
        slot_row = iota((128 * SLOT, 2 * PAN), 0)

        def pick(g, carry):
            hot = (slot_row == slots[pl.ds(g, 1), :]).astype(f32).astype(bf16)
            picked[g] = nn(turned[: RHS * EQ, :], hot).astype(bf16)
            return carry

        lax.fori_loop(0, slots.shape[0], pick, 0)

        def build(g, half, per, base):
            ids = kinds[pl.ds(g, 1), :][:, PAN * half : PAN * (half + 1)]
            kind = jnp.broadcast_to(ids, (PAN, PAN)).T
            src = picked[g, :, PAN * half : PAN * (half + 1)]
            for h in range(0, per, 2):
                hot = jnp.concatenate(
                    [
                        (kind == iota((PAN, PAN), 1) + (PAN * t + h * OPSP)).astype(f32).astype(bf16)
                        for t in range(6)
                    ],
                    1,
                )
                y = nn(src, hot)
                for r in range(RHS):
                    for u in range(2):
                        at = pl.multiple_of((base + r * LEAF + h + u) * EQ, 8)
                        for t in range(3):
                            spread[t][pl.ds(at, EQ), :] = y[
                                r * EQ : (r + 1) * EQ, PAN * (t + 3 * u) : PAN * (t + 3 * u + 1)
                            ]

        def far_group(g, carry):
            build(g, 0, 2, g * 4)
            build(g, 1, 2, g * 4 + 2)
            return carry

        def top_group(g, carry):
            build(g, 0, 4, ROWS + (g - 4) * 8)
            build(g, 1, 4, ROWS + (g - 4) * 8 + 4)
            return carry

        lax.fori_loop(0, 4, far_group, 0)
        lax.fori_loop(4, 6, top_group, 0)

    def move(to):
        for h, ops in enumerate((ops0, ops1)):
            rows = ops.shape[0] * 8
            for g in range(FB // 8):
                at = slice(g * 8 * EQ + h * rows, g * 8 * EQ + (h + 1) * rows)
                part = ops[:, 8 * g : 8 * g + 8, :].astype(f32).reshape(rows, ops.shape[2])
                for t in range(2):
                    to[t][at, :] = part[:, PAN * t : PAN * (t + 1)]
                to[2][at, :tail] = part[:, 2 * PAN :]

    def multiply(width, of):
        base = (step - 1) * FB
        left = []
        right = []
        for i in range(width):
            for t in range(3):
                left.append(spread[t][pl.ds(base + i, 2 * ROWS, stride=EQ), :].astype(bf16))
                right.append(of[t][pl.ds(i // 8 * 8 * EQ + i % 8, EQ, stride=8), :].astype(bf16))
        acc[...] += nt(jnp.concatenate(right, 1), jnp.concatenate(left, 1))

    last = pl.num_programs(0) - 1

    @pl.when(step == 0)
    def _():
        move(even)

    @pl.when((step > 0) & (step < last) & (step % 2 == 1))
    def _():
        multiply(FB, even)
        move(odd)

    @pl.when((step > 0) & (step < last) & (step % 2 == 0))
    def _():
        multiply(FB, odd)
        move(even)

    @pl.when(step == last)
    def _():
        multiply(EQ % FB, odd)
        res = acc[...].T
        far = res[:ROWS]
        top = res[ROWS:].astype(bf16)
        row = iota((ROWS, ROWS), 0)
        lane = iota((ROWS, ROWS), 1)
        parent = jnp.zeros((ROWS, ROWS), i32)
        for n in range(LEAF):
            parent = jnp.where(row % LEAF == n, par[0, n], parent)
        hit = (parent == lane % LEAF) & (row // LEAF == lane // LEAF)
        chosen = nn(hit.astype(f32).astype(bf16), top).astype(bf16)
        leaf_row = iota((ROWS, EQ), 0) % LEAF
        down = jnp.zeros((ROWS, EQ), f32)
        for n in range(LEAF):
            down = jnp.where(leaf_row == n, nt(chosen, l2l[octs[0, n]]), down)
        local = (down + far).astype(bf16)
        leaf_row = iota((ROWS, PAN), 0) % LEAF
        res = jnp.zeros((ROWS, PAN), f32)
        for n in range(LEAF):
            res = jnp.where(leaf_row == n, nn(local, tp[n]), res)
        out[...] = res + near_part[...]


def finish(par, octs, slots, kinds, arrived, tables, l2l, tp, near_part):
    chunks = pl.cdiv(EQ, FB)
    half = (EQ // 2, FB, tables.shape[2])
    return pl.pallas_call(
        finish_kernel,
        grid=(chunks + 1,),
        in_specs=[
            SM,
            SM,
            whole(slots),
            whole(kinds),
            whole(arrived),
            pl.BlockSpec(half, lambda i: (0, jnp.minimum(i, chunks - 1), 0)),
            pl.BlockSpec(half, lambda i: (1, jnp.minimum(i, chunks - 1), 0)),
            whole(l2l),
            whole(tp),
            whole(near_part),
        ],
        out_specs=pl.BlockSpec((ROWS, PAN), lambda i: (0, 0)),
        out_shape=jax.ShapeDtypeStruct((ROWS, PAN), f32),
        scratch_shapes=[
            pltpu.VMEM((BOX, 128 * SLOT), bf16),
            pltpu.VMEM((6, RHS * EQ, 2 * PAN), bf16),
            pltpu.VMEM((2 * ROWS * EQ, PAN), f32),
            pltpu.VMEM((2 * ROWS * EQ, PAN), f32),
            pltpu.VMEM((2 * ROWS * EQ, PAN), f32),
            pltpu.VMEM((EQ * FB, PAN), f32),
            pltpu.VMEM((EQ * FB, PAN), f32),
            pltpu.VMEM((EQ * FB, PAN), f32),
            pltpu.VMEM((EQ * FB, PAN), f32),
            pltpu.VMEM((EQ * FB, PAN), f32),
            pltpu.VMEM((EQ * FB, PAN), f32),
            pltpu.VMEM((EQ, 2 * ROWS), f32),
        ],
        compiler_params=pltpu.CompilerParams(vmem_limit_bytes=BIG),
        name="finish",
    )(par, octs, slots, kinds, arrived, tables, tables, l2l, tp, near_part)


def per_device(
    density,
    centres,
    normal,
    to_multipole,
    to_panels,
    m2m_ops,
    l2l_ops,
    m2l_ops,
    near_index,
    near_count,
    send_box,
    send_count,
    far_slot,
    far_op,
    far_count,
    parent_of,
    octant,
    top_src,
    top_op,
    top_count,
):
    dens = density.reshape(ROWS, PAN)
    mult, part, low, high = upward(parent_of, octant, dens, centres, normal, to_multipole, m2m_ops)

    axes = ("leaf", "sub")
    count = lax.axis_size("leaf") * lax.axis_size("sub")
    forward = [(i, i + 1) for i in range(count - 1)]
    backward = [(i + 1, i) for i in range(count - 1)]
    low = lax.ppermute(low, axes, forward)
    high = lax.ppermute(high, axes, backward)

    pieces = lax.all_to_all(part, "sub", split_axis=0, concat_axis=0, tiled=True)

    slot_id = jnp.arange(2, dtype=i32)[None, :]
    far_ids = jnp.where(slot_id < send_count[0][:, None], send_box[0], -1)
    own_ids = jnp.broadcast_to(
        jnp.array([16, 17, 18, 19, -1, -1], i32)[None, :], (count, SLOT - 2)
    )
    ids = jnp.concatenate([far_ids, own_ids], 1).reshape(count * SLOT, 1)
    outgoing = pack(ids, mult, pieces)
    arrived = lax.all_to_all(outgoing, axes, split_axis=0, concat_axis=0, tiled=True)

    near_part = near(near_index, near_count, centres, normal, dens, low, high)

    far_live = jnp.arange(far_slot.shape[1])[None, :] < far_count[:, None]
    far_rows = jnp.where(far_live, (far_slot // 2) * SLOT + far_slot % 2, -1)
    top_live = jnp.arange(top_src.shape[1])[None, :] < top_count[:, None]
    top_rows = jnp.where(top_live, (top_src // 4) * SLOT + 2 + top_src % 4, -1)
    slots = jnp.concatenate([far_rows.reshape(4, 2 * PAN), top_rows.reshape(2, 2 * PAN)], 0)
    far_kind = far_op + OPSP * (jnp.arange(LEAF, dtype=i32) % 2)[:, None]
    top_kind = top_op + OPSP * (jnp.arange(LEAF, dtype=i32) % 4)[:, None]
    kinds = jnp.concatenate([far_kind.reshape(4, 2 * PAN), top_kind.reshape(2, 2 * PAN)], 0)

    res = finish(
        parent_of,
        octant,
        slots,
        kinds,
        arrived,
        jnp.transpose(m2l_ops, (1, 2, 0)),
        l2l_ops,
        jnp.transpose(to_panels, (0, 2, 1)),
        near_part,
    )
    return res.reshape(RHS, LEAF, PAN)


def solution(mesh):
    both = ("leaf", "sub")
    return jax.shard_map(
        per_device,
        mesh=mesh,
        in_specs=(
            P(None, both, None),
            P(None, both, None),
            P(None, both, None),
            P(both, None, None),
            P(both, None, None),
            P(),
            P(),
            P(),
            P(both, None),
            P(both),
            P(both, None, None),
            P(both, None),
            P(both, None),
            P(both, None),
            P(both),
            P("leaf", "sub"),
            P("leaf", "sub"),
            P("leaf", None),
            P("leaf", None),
            P("leaf"),
        ),
        out_specs=P(None, both, None),
        check_vma=False,
    )
```

time: 147 us -> 83.8 us (0.57)
  the two profiles are of different devices: /device:TPU:101 before, /device:TPU:1 now
where the time goes in v1:
time: 83.8 us; the launch traced here: 83.2 us
  Pallas kernels  48.9 us (58%)
  starting transfers between devices  21.7 us (26%)
  waiting for transfers between devices  7.03 us (8%)
  local copies, waits for them, and re-layouts  4.42 us (5%)
  other arithmetic  0.99 us (1%)
    pallas_call x1, Pallas kernels, finish(): pl.pallas_call(finish_kernel, grid=(chunks + 1,), in_specs=[SM, SM, whole...  26.6 us
    pallas_call x1, Pallas kernels, near(): pl.pallas_call(near_kernel, grid=(1,), in_specs=[SM, SM] + [whole(x) for...  16.1 us
    all_to_all x1, starting transfers between devices, per_device(): lax.all_to_all(outgoing, axes, split_axis=0, concat_axis=0, tiled=True)  10.8 us
    ppermute x1, starting transfers between devices, per_device(): low = lax.ppermute(low, axes, forward)  3.94 us
    all_to_all x1, waiting for transfers between devices, per_device(): lax.all_to_all(outgoing, axes, split_axis=0, concat_axis=0, tiled=True)  3.85 us
    ppermute x1, starting transfers between devices, per_device(): high = lax.ppermute(high, axes, backward)  3.74 us
    all_to_all x1, starting transfers between devices, per_device(): lax.all_to_all(part, 'sub', split_axis=0, concat_axis=0, tiled=True)  3.29 us
    pallas_call x1, Pallas kernels, upward(): pl.pallas_call(upward_kernel, grid=(1,), in_specs=[SM, SM] + [whole(x) fo...  3.29 us
  transfers between devices with their start and end apart: 4, of which 2 were waited for; matrix products, arithmetic and copies ran while one was open for 3% of the time, Pallas kernels for 23%

profile of v1, /device:TPU:1, one launch (start us, length us, event | category | flops | bytes accessed | tf_op | source)
XLA Modules:
  0.0 83.2 jit_solution(1395284426253507356)
XLA Ops:
  0.0 3.3 %upward.1 = (bf16[64,152]{1,0:T(8,128)(2,1)}, f32[64,152]{1,0:T(8,128)}, f32[40,128]{1,0:T(8,128)}, f32[40,128]{1,0:T(8,128)}) custom-call(s32[1,16]{1,0:T(1,128)} %par.3, s32[1,16]{1,0:T(1,128)} %octs.3, f32[64,128]{1,0:T(8,128)} %bitcast.18, f32[3,16,128]{2,1,0:T(8,128)} %cen.3, f32[3,16,128]{2,1,0:T(8,128)} %nrm.3, bf16[16,152,128]{2,1,0:T(8,128)(2,1)} %tm.1, ...), custom_call_target="tpu_custom_call" | custom-call | tf_op jit(solution)/shard_map/upward/pallas_call | solution.py:81
  3.3 3.9 %collective-permute-start = (f32[40,128]{1,0:T(8,128)}, f32[40,128]{1,0:T(8,128)S(1)}, u32[]{:S(2)}, u32[]{:S(2)}) collective-permute-start(f32[40,128]{1,0:T(8,128)} %get-tuple-element.11), channel_id=1, source_target_pairs={{0,1},{1,2},{2,3},{3,4},{4,5},{5,6},{6,7},{7,8},{8,9},{9,10},{10,1... | collective-permute-start | bytes 61448 | tf_op jit(solution)/shard_map/ppermute | solution.py:449
  7.2 3.7 %collective-permute-start.1 = (f32[40,128]{1,0:T(8,128)}, f32[40,128]{1,0:T(8,128)S(1)}, u32[]{:S(2)}, u32[]{:S(2)}) collective-permute-start(f32[40,128]{1,0:T(8,128)} %get-tuple-element.12), channel_id=1, source_target_pairs={{1,0},{2,1},{3,2},{4,3},{5,4},{6,5},{7,6},{8,7},{9,8},{10,9},{11,1... | collective-permute-start | bytes 61448 | tf_op jit(solution)/shard_map/ppermute | solution.py:450
  11.0 3.3 %all-to-all-start = ((f32[4,16,152]{2,1,0:T(8,128)}), f32[4,16,152]{2,1,0:T(8,128)S(1)}, u32[]{:S(2)}, u32[]{:S(2)}) async-start(f32[4,16,152]{2,1,0:T(8,128)} %bitcast.17), calls=%async_computation | async-start | bytes 131072 | tf_op jit(solution)/shard_map/all_to_all | solution.py:452
  14.3 0.1 pad.1.clone
  14.4 0.1 pad_add_fusion.2
  14.5 0.1 copy.25
  14.6 1.0 %reshape.58.ids = s32[1024,1]{1,0:T(8,128)} reshape(s32[128,8]{1,0:T(8,128)S(1)} %copy.25) | data formatting | bytes 8192 | tf_op jit(solution)/shard_map/reshape | solution.py:459
  15.6 3.2 %all-to-all-done = f32[4,16,152]{2,1,0:T(8,128)S(1)} async-done(((f32[4,16,152]{2,1,0:T(8,128)}), f32[4,16,152]{2,1,0:T(8,128)S(1)}, u32[]{:S(2)}, u32[]{:S(2)}) %all-to-all-start) | async-done | bytes 38944 | tf_op jit(solution)/shard_map/all_to_all | solution.py:452
  18.7 0.6 copy-done.1
  19.4 2.9 %pack.1 = bf16[1024,640]{1,0:T(8,128)(2,1)} custom-call(s32[1024,1]{1,0:T(8,128)} %reshape.58.ids, bf16[64,152]{1,0:T(8,128)(2,1)} %get-tuple-element.9.mult, f32[64,152]{1,0:T(8,128)} %bitcast.16), custom_call_target="tpu_custom_call" | custom-call | tf_op jit(solution)/shard_map/pack/pallas_call | solution.py:113
  22.3 0.0 copy-start.5
  22.3 0.0 copy-start.9
  22.3 10.8 %all-to-all-start.1 = ((bf16[128,8,640]{2,1,0:T(8,128)(2,1)}), bf16[128,8,640]{2,1,0:T(8,128)(2,1)S(1)}, u32[]{:S(2)}, u32[]{:S(2)}) async-start(bf16[128,8,640]{2,1,0:T(8,128)(2,1)} %bitcast.14), calls=%async_computation.1 | async-start | bytes 2621440 | tf_op jit(solution)/shard_map/all_to_all | solution.py:461
  33.1 0.1 broadcast_add_fusion.1
  33.1 0.1 reshape.53
  33.2 0.0 copy-done.3
  33.2 0.1 fusion.2
  33.3 0.1 reshape.51
  33.4 0.1 broadcast_add_fusion
  33.5 0.1 reshape.54
  33.5 0.1 fusion.6
  33.6 0.1 reshape.52
  33.7 0.6 pad_add_fusion
  34.3 0.0 collective-permute-done.low
  34.3 0.0 collective-permute-done.1.high
  34.3 0.6 copy-done.10
  34.9 0.6 copy-done.11
  35.5 16.1 %near.1.near_part = f32[64,128]{1,0:T(8,128)} custom-call(s32[16,27]{1,0:T(8,128)} %index.1, s32[16]{0:T(128)} %count.1, f32[3,16,128]{2,1,0:T(8,128)} %cen.3, f32[3,16,128]{2,1,0:T(8,128)} %nrm.3, f32[64,128]{1,0:T(8,128)} %bitcast.19, f32[40,128]{1,0:T(8,128)} %copy-done.10, f32[40,128]{1,0:T(8,128)} %copy-done.11), custom_call_target="tpu_custom_call" | custom-call | flops 2000000000 | bytes 1000000 | tf_op jit(solution)/shard_map/near/pallas_call | solution.py:235
  51.6 3.9 %all-to-all-done.1 = bf16[128,8,640]{2,1,0:T(8,128)(2,1)S(1)} async-done(((bf16[128,8,640]{2,1,0:T(8,128)(2,1)}), bf16[128,8,640]{2,1,0:T(8,128)(2,1)S(1)}, u32[]{:S(2)}, u32[]{:S(2)}) %all-to-all-start.1) | async-done | bytes 1310752 | tf_op jit(solution)/shard_map/all_to_all | solution.py:461
  55.5 1.1 %copy-done = bf16[128,8,640]{2,1,0:T(8,128)(2,1)} copy-done((bf16[128,8,640]{2,1,0:T(8,128)(2,1)}, bf16[128,8,640]{2,1,0:T(8,128)(2,1)S(1)}, u32[]{:S(2)}) %copy-start) | copy-done | bytes 1310744
  56.5 26.6 %finish.1 = f32[64,128]{1,0:T(8,128)} custom-call(s32[1,16]{1,0:T(1,128)} %par.3, s32[1,16]{1,0:T(1,128)} %octs.3, s32[6,256]{1,0:T(8,128)} %get-tuple-element.13.slots, s32[6,256]{1,0:T(8,128)} %get-tuple-element.14.kinds, bf16[1024,640]{1,0:T(8,128)(2,1)} %bitcast.13, bf16[152,152,316]{2,1,0:T(8,128)(2,1)} %bitcast.11, bf16[152,152,316]{2,1,0:T(8,128)(2,1)} %bitcast.12, ...), custom_call_target="tpu_custom_call" | custom-call | tf_op jit(solution)/shard_map/finish/pallas_call | solution.py:384
  (22 shorter events, 0.0 us)
Async XLA Ops:
  0.0 14.3 %copy-start.12 = (s32[6]{0:T(128)S(1)}, s32[6]{0:T(128)}, u32[]{:S(2)}) copy-start(s32[6]{0:T(128)} %constant.74.clone) | copy-start | bytes 76
  0.0 14.3 %copy-start.7 = (s32[1,128]{1,0:T(1,128)S(1)}, s32[1,128]{1,0:T(1,128)}, u32[]{:S(2)}) copy-start(s32[1,128]{1,0:T(1,128)} %param.32) | copy-start | bytes 1540
  0.0 14.3 %copy-start.6 = (s32[1,128,2]{1,2,0:T(2,128)S(1)}, s32[1,128,2]{1,2,0:T(2,128)}, u32[]{:S(2)}) copy-start(s32[1,128,2]{1,2,0:T(2,128)} %param.31) | copy-start | bytes 3076
  3.3 31.0 %collective-permute-start = (f32[40,128]{1,0:T(8,128)}, f32[40,128]{1,0:T(8,128)S(1)}, u32[]{:S(2)}, u32[]{:S(2)}) collective-permute-start(f32[40,128]{1,0:T(8,128)} %get-tuple-element.11), channel_id=1, source_target_pairs={{0,1},{1,2},{2,3},{3,4},{4,5},{5,6},{6,7},{7,8},{8,9},{9,10},{10,1... | collective-permute-start | bytes 61448 | tf_op jit(solution)/shard_map/ppermute | solution.py:449
  7.2 27.1 %collective-permute-start.1 = (f32[40,128]{1,0:T(8,128)}, f32[40,128]{1,0:T(8,128)S(1)}, u32[]{:S(2)}, u32[]{:S(2)}) collective-permute-start(f32[40,128]{1,0:T(8,128)} %get-tuple-element.12), channel_id=1, source_target_pairs={{1,0},{2,1},{3,2},{4,3},{5,4},{6,5},{7,6},{8,7},{9,8},{10,9},{11,1... | collective-permute-start | bytes 61448 | tf_op jit(solution)/shard_map/ppermute | solution.py:450
  11.0 7.7 %all-to-all-start = ((f32[4,16,152]{2,1,0:T(8,128)}), f32[4,16,152]{2,1,0:T(8,128)S(1)}, u32[]{:S(2)}, u32[]{:S(2)}) async-start(f32[4,16,152]{2,1,0:T(8,128)} %bitcast.17), calls=%async_computation | async-start | bytes 131072 | tf_op jit(solution)/shard_map/all_to_all | solution.py:452
  18.7 0.6 copy-start.1
  22.2 10.8 %copy-start.2 = (s32[16,64]{1,0:T(8,128)S(1)}, s32[16,64]{1,0:T(8,128)}, u32[]{:S(2)}) copy-start(s32[16,64]{1,0:T(8,128)} %param.34) | copy-start | bytes 12292
  22.2 11.0 %copy-start.3 = (s32[16,64]{1,0:T(8,128)S(1)}, s32[16,64]{1,0:T(8,128)}, u32[]{:S(2)}) copy-start(s32[16,64]{1,0:T(8,128)} %param.33) | copy-start | bytes 12292
  22.2 11.0 %copy-start.8 = (s32[16]{0:T(128)S(1)}, s32[16]{0:T(128)}, u32[]{:S(2)}) copy-start(s32[16]{0:T(128)} %param.35) | copy-start | bytes 196
  22.2 11.1 %copy-start.4 = (s32[16,32]{1,0:T(8,128)S(1)}, s32[16,32]{1,0:T(8,128)}, u32[]{:S(2)}) copy-start(s32[16,32]{1,0:T(8,128)} %param.39) | copy-start | bytes 6148
  22.3 11.3 %copy-start.5 = (s32[16,32]{1,0:T(8,128)S(1)}, s32[16,32]{1,0:T(8,128)}, u32[]{:S(2)}) copy-start(s32[16,32]{1,0:T(8,128)} %param.38) | copy-start | bytes 6148
  22.3 11.3 %copy-start.9 = (s32[16]{0:T(128)S(1)}, s32[16]{0:T(128)}, u32[]{:S(2)}) copy-start(s32[16]{0:T(128)} %param.40) | copy-start | bytes 196
  22.3 33.2 %all-to-all-start.1 = ((bf16[128,8,640]{2,1,0:T(8,128)(2,1)}), bf16[128,8,640]{2,1,0:T(8,128)(2,1)S(1)}, u32[]{:S(2)}, u32[]{:S(2)}) async-start(bf16[128,8,640]{2,1,0:T(8,128)(2,1)} %bitcast.14), calls=%async_computation.1 | async-start | bytes 2621440 | tf_op jit(solution)/shard_map/all_to_all | solution.py:461
  34.3 0.6 copy-start.10
  34.9 0.6 copy-start.11
  55.5 1.1 %copy-start = (bf16[128,8,640]{2,1,0:T(8,128)(2,1)}, bf16[128,8,640]{2,1,0:T(8,128)(2,1)S(1)}, u32[]{:S(2)}) copy-start(bf16[128,8,640]{2,1,0:T(8,128)(2,1)S(1)} %all-to-all-done.1) | copy-start | bytes 3932164

commit v2 on v1

--- a/solution.py
+++ b/solution.py
@@ -17,7 +17,9 @@
 OPSP = 384
 PAN = 128
 BOX = 640
-SLOT = 8
+PIECES = 5
+CHUNK = 32
+PITCH = 40
 EPS = 0.01
 FB = 16
 MIB = 1 << 20
@@ -42,7 +44,7 @@
     return lax.broadcasted_iota(i32, shape, dim)
 
 
-def upward_kernel(par, octs, dens, cen, nrm, tm, m2m, mult_out, part_out, low_out, high_out):
+def upward_kernel(par, octs, dens, cen, nrm, tm, m2m, mult_out, c0, c1, c2, c3, low_out, high_out):
     d = dens[...].astype(bf16)
     leaf_row = iota((ROWS, EQ), 0) % LEAF
     mult = jnp.zeros((ROWS, EQ), f32)
@@ -58,9 +60,11 @@
     parent = jnp.zeros((ROWS, ROWS), i32)
     for n in range(LEAF):
         parent = jnp.where(lane % LEAF == n, par[0, n], parent)
-    box = (row // 16) * 4 + row % 4
+    box = ((row // 16 + lax.axis_index("sub")) % 4) * 4 + row % 4
     hit = (parent == box) & ((row // 4) % 4 == lane // LEAF)
-    part_out[...] = nn(hit.astype(f32), child, precision=lax.Precision.HIGHEST)
+    part = nn(hit.astype(f32), child, precision=lax.Precision.HIGHEST)
+    for s, piece in enumerate((c0, c1, c2, c3)):
+        piece[...] = part[16 * s : 16 * s + 16]
     for a in range(3):
         high_out[4 * a : 4 * a + 4, :] = cen[a, :RIM, :]
         low_out[4 * a : 4 * a + 4, :] = cen[a, LEAF - RIM :, :]
@@ -69,15 +73,12 @@
     for r in range(RHS):
         high_out[24 + 4 * r : 28 + 4 * r, :] = dens[LEAF * r : LEAF * r + RIM, :]
         low_out[24 + 4 * r : 28 + 4 * r, :] = dens[LEAF * (r + 1) - RIM : LEAF * (r + 1), :]
-
-
 def upward(par, octs, dens, cen, nrm, tm, m2m):
     outs = [
         jax.ShapeDtypeStruct((ROWS, EQ), bf16),
-        jax.ShapeDtypeStruct((ROWS, EQ), f32),
-        jax.ShapeDtypeStruct((40, PAN), f32),
-        jax.ShapeDtypeStruct((40, PAN), f32),
     ]
+    outs += [jax.ShapeDtypeStruct((16, EQ), f32)] * 4
+    outs += [jax.ShapeDtypeStruct((40, PAN), f32)] * 2
     return pl.pallas_call(
         upward_kernel,
         grid=(1,),
@@ -89,12 +90,10 @@
     )(par, octs, dens, cen, nrm, tm, m2m)
 
 
-def pack_kernel(ids, mult, pieces, out):
+def pack_kernel(boxes, counts, mult, c0, c1, c2, c3, low, high, out, far, const):
     row = iota((EQ, BOX), 0)
     lane = iota((EQ, BOX), 1)
-    own = pieces[0:16, :]
-    for s in range(1, 4):
-        own = own + pieces[16 * s : 16 * s + 16, :]
+    own = (c0[...] + c1[...]) + (c2[...] + c3[...])
     own = own.astype(bf16).astype(f32)
     mf = mult[...].astype(f32)
     table = jnp.zeros((24, BOX), f32)
@@ -104,21 +103,40 @@
         )
         place = (lane == row + EQ * r).astype(f32).astype(bf16)
         table = table + nn(both.astype(bf16), place)
-    hot = (ids[...] == iota((128 * SLOT, 24), 1)).astype(f32).astype(bf16)
-    out[...] = nn(hot, table.astype(bf16)).astype(bf16)
-
-
-def pack(ids, mult, pieces):
-    outs = jax.ShapeDtypeStruct((128 * SLOT, BOX), bf16)
+    leaf = iota((LEAF, PAN), 0)
+    for j in range(2):
+        hot = ((boxes[j : j + 1, :] == leaf) & (counts[...] > j)).astype(f32).T
+        y = nn(hot.astype(bf16), table[:LEAF].astype(bf16))
+        for t in range(PIECES):
+            far[pl.ds(PIECES * j + t, PAN, stride=24), :] = y[:, PAN * t : PAN * (t + 1)]
+    const[...] = jnp.zeros_like(const)
+    for q in range(4):
+        for t in range(PIECES):
+            at = PIECES * (2 + q) + t
+            const[at : at + 1, :] = table[LEAF + q : LEAF + q + 1, PAN * t : PAN * (t + 1)]
+    head = const[:16]
+    rest = const[16:].astype(bf16)
+    is_far = iota((16, PAN), 0) < 2 * PIECES
+    for d in range(PAN):
+        out[CHUNK * d : CHUNK * d + 16, :] = jnp.where(
+            is_far, far[24 * d : 24 * d + 16, :], head
+        ).astype(bf16)
+        out[CHUNK * d + 16 : CHUNK * (d + 1), :] = rest
+
+
+def pack(boxes, counts, mult, pieces, later):
+    outs = jax.ShapeDtypeStruct((PAN * CHUNK, PAN), bf16)
     return pl.pallas_call(
         pack_kernel,
         grid=(1,),
-        in_specs=[whole(x) for x in (ids, mult, pieces)],
+        in_specs=[whole(x) for x in (boxes, counts, mult, *pieces)]
+        + [pl.BlockSpec(memory_space=pl.ANY)] * len(later),
         out_specs=whole(outs),
         out_shape=outs,
+        scratch_shapes=[pltpu.VMEM((PAN * 24, PAN), f32), pltpu.VMEM((CHUNK, PAN), f32)],
         compiler_params=pltpu.CompilerParams(vmem_limit_bytes=BIG),
         name="pack",
-    )(ids, mult, pieces)
+    )(boxes, counts, mult, *pieces, *later)
 
 
 SRC = LEAF + 2 * RIM
@@ -258,8 +276,8 @@
 
 
 def finish_kernel(
-    par, octs, slots, kinds, arrived, ops0, ops1, l2l, tp, near_part, out,
-    turned, picked, s0, s1, s2, m0, m1, m2, m3, m4, m5, acc,
+    par, octs, far_count, top_count, far_slot, far_op, top_src, top_op, arrived, ops0, ops1, l2l, tp, near_part, out,
+    ids, slots, kinds, turned, picked, s0, s1, s2, m0, m1, m2, m3, m4, m5, acc,
 ):
     step = pl.program_id(0)
     spread = (s0, s1, s2)
@@ -272,16 +290,47 @@
         acc[...] = jnp.zeros_like(acc)
         m2[...] = jnp.zeros_like(m2)
         m5[...] = jnp.zeros_like(m5)
-        for t in range(BOX // PAN):
-            turned[PAN * t : PAN * (t + 1), :] = arrived[:, PAN * t : PAN * (t + 1)].T
-        slot_row = iota((128 * SLOT, 2 * PAN), 0)
-
-        def pick(g, carry):
-            hot = (slot_row == slots[pl.ds(g, 1), :]).astype(f32).astype(bf16)
-            picked[g] = nn(turned[: RHS * EQ, :], hot).astype(bf16)
-            return carry
-
-        lax.fori_loop(0, slots.shape[0], pick, 0)
+        for p in range(PAN):
+            s0[PITCH * p : PITCH * p + CHUNK, :] = arrived[CHUNK * p : CHUNK * (p + 1), :].astype(f32)
+        for j in range(6):
+            for t in range(PIECES):
+                piece = s0[pl.ds(PIECES * j + t, PAN, stride=PITCH), :].T
+                turned[PAN * t : PAN * (t + 1), PAN * j : PAN * (j + 1)] = piece.astype(bf16)
+
+        row = iota((LEAF, far_slot.shape[1]), 0)
+        lane = iota((LEAF, far_slot.shape[1]), 1)
+        live = jnp.zeros(row.shape, i32)
+        for n in range(LEAF):
+            live = jnp.where(row == n, far_count[n], live)
+        slot = far_slot[...]
+        ids[...] = jnp.where(lane < live, (slot % 2) * PAN + slot // 2, -1)
+        slots[0:4, :] = jnp.concatenate([ids[pl.ds(h, 4, stride=4), :] for h in range(4)], 1)
+        kinds[0:4, :] = jnp.concatenate(
+            [far_op[pl.ds(h, 4, stride=4), :] + OPSP * (h % 2) for h in range(4)], 1
+        )
+        row = iota((LEAF, top_src.shape[1]), 0)
+        lane = iota((LEAF, top_src.shape[1]), 1)
+        live = jnp.zeros(row.shape, i32)
+        for n in range(LEAF):
+            live = jnp.where(row == n, top_count[n], live)
+        slot = top_src[...]
+        ids[:, : row.shape[1]] = jnp.where(lane < live, (slot % 4) * PAN + slot // 4, -1)
+        slots[4:6, :] = jnp.concatenate(
+            [ids[pl.ds(h, 2, stride=8), :][:, : row.shape[1]] for h in range(8)], 1
+        )
+        kinds[4:6, :] = jnp.concatenate(
+            [top_op[pl.ds(h, 2, stride=8), :] + OPSP * (h % 4) for h in range(8)], 1
+        )
+        far_row = iota((2 * PAN, 2 * PAN), 0)
+        top_row = iota((4 * PAN, 2 * PAN), 0)
+        for g in range(6):
+            if g < 4:
+                hot = (far_row == slots[g : g + 1, :]).astype(f32).astype(bf16)
+                table = turned[: RHS * EQ, : 2 * PAN]
+            else:
+                hot = (top_row == slots[g : g + 1, :]).astype(f32).astype(bf16)
+                table = turned[: RHS * EQ, 2 * PAN :]
+            picked[g] = nn(table, hot).astype(bf16)
 
         def build(g, half, per, base):
             ids = kinds[pl.ds(g, 1), :][:, PAN * half : PAN * (half + 1)]
@@ -378,7 +427,7 @@
         out[...] = res + near_part[...]
 
 
-def finish(par, octs, slots, kinds, arrived, tables, l2l, tp, near_part):
+def finish(par, octs, far_count, top_count, far_slot, far_op, top_src, top_op, arrived, tables, l2l, tp, near_part):
     chunks = pl.cdiv(EQ, FB)
     half = (EQ // 2, FB, tables.shape[2])
     return pl.pallas_call(
@@ -387,8 +436,12 @@
         in_specs=[
             SM,
             SM,
-            whole(slots),
-            whole(kinds),
+            SM,
+            SM,
+            whole(far_slot),
+            whole(far_op),
+            whole(top_src),
+            whole(top_op),
             whole(arrived),
             pl.BlockSpec(half, lambda i: (0, jnp.minimum(i, chunks - 1), 0)),
             pl.BlockSpec(half, lambda i: (1, jnp.minimum(i, chunks - 1), 0)),
@@ -399,7 +452,10 @@
         out_specs=pl.BlockSpec((ROWS, PAN), lambda i: (0, 0)),
         out_shape=jax.ShapeDtypeStruct((ROWS, PAN), f32),
         scratch_shapes=[
-            pltpu.VMEM((BOX, 128 * SLOT), bf16),
+            pltpu.VMEM((LEAF, 64), i32),
+            pltpu.VMEM((8, 2 * PAN), i32),
+            pltpu.VMEM((8, 2 * PAN), i32),
+            pltpu.VMEM((BOX, 6 * PAN), bf16),
             pltpu.VMEM((6, RHS * EQ, 2 * PAN), bf16),
             pltpu.VMEM((2 * ROWS * EQ, PAN), f32),
             pltpu.VMEM((2 * ROWS * EQ, PAN), f32),
@@ -414,7 +470,7 @@
         ],
         compiler_params=pltpu.CompilerParams(vmem_limit_bytes=BIG),
         name="finish",
-    )(par, octs, slots, kinds, arrived, tables, tables, l2l, tp, near_part)
+    )(par, octs, far_count, top_count, far_slot, far_op, top_src, top_op, arrived, tables, tables, l2l, tp, near_part)
 
 
 def per_device(
@@ -440,7 +496,13 @@
     top_count,
 ):
     dens = density.reshape(ROWS, PAN)
-    mult, part, low, high = upward(parent_of, octant, dens, centres, normal, to_multipole, m2m_ops)
+    mult, own, *others, low, high = upward(
+        parent_of, octant, dens, centres, normal, to_multipole, m2m_ops
+    )
+    subs = lax.axis_size("sub")
+    pieces = [own]
+    for s, piece in enumerate(others, 1):
+        pieces.append(lax.ppermute(piece, "sub", [(i, (i + s) % subs) for i in range(subs)]))
 
     axes = ("leaf", "sub")
     count = lax.axis_size("leaf") * lax.axis_size("sub")
@@ -449,34 +511,23 @@
     low = lax.ppermute(low, axes, forward)
     high = lax.ppermute(high, axes, backward)
 
-    pieces = lax.all_to_all(part, "sub", split_axis=0, concat_axis=0, tiled=True)
-
-    slot_id = jnp.arange(2, dtype=i32)[None, :]
-    far_ids = jnp.where(slot_id < send_count[0][:, None], send_box[0], -1)
-    own_ids = jnp.broadcast_to(
-        jnp.array([16, 17, 18, 19, -1, -1], i32)[None, :], (count, SLOT - 2)
+    outgoing = pack(jnp.transpose(send_box[0]), send_count, mult, pieces, (low, high))
+    arrived = lax.all_to_all(
+        outgoing.reshape(count, CHUNK, PAN), axes, split_axis=0, concat_axis=0, tiled=True
     )
-    ids = jnp.concatenate([far_ids, own_ids], 1).reshape(count * SLOT, 1)
-    outgoing = pack(ids, mult, pieces)
-    arrived = lax.all_to_all(outgoing, axes, split_axis=0, concat_axis=0, tiled=True)
 
     near_part = near(near_index, near_count, centres, normal, dens, low, high)
-
-    far_live = jnp.arange(far_slot.shape[1])[None, :] < far_count[:, None]
-    far_rows = jnp.where(far_live, (far_slot // 2) * SLOT + far_slot % 2, -1)
-    top_live = jnp.arange(top_src.shape[1])[None, :] < top_count[:, None]
-    top_rows = jnp.where(top_live, (top_src // 4) * SLOT + 2 + top_src % 4, -1)
-    slots = jnp.concatenate([far_rows.reshape(4, 2 * PAN), top_rows.reshape(2, 2 * PAN)], 0)
-    far_kind = far_op + OPSP * (jnp.arange(LEAF, dtype=i32) % 2)[:, None]
-    top_kind = top_op + OPSP * (jnp.arange(LEAF, dtype=i32) % 4)[:, None]
-    kinds = jnp.concatenate([far_kind.reshape(4, 2 * PAN), top_kind.reshape(2, 2 * PAN)], 0)
 
     res = finish(
         parent_of,
         octant,
-        slots,
-        kinds,
-        arrived,
+        far_count,
+        top_count,
+        far_slot,
+        far_op,
+        top_src,
+        top_op,
+        arrived.reshape(count * CHUNK, PAN),
         jnp.transpose(m2l_ops, (1, 2, 0)),
         l2l_ops,
         jnp.transpose(to_panels, (0, 2, 1)),

time: 83.8 us -> 77 us (0.919)
  Pallas kernels: 48.9 us -> 44.9 us
  local copies, waits for them, and re-layouts: 4.42 us -> 1.55 us
  starting transfers between devices: 21.7 us -> 22.9 us
  other arithmetic: 0.99 us -> 0 us
    ppermute x0 -> x3, starting transfers between devices: none -> 3.3 us  [per_device(): lax.ppermute(piece, 'sub', [(i, (i + s) % subs) for i in range(subs)])]
    pallas_call x2, Pallas kernels: 29.5 us -> 26.8 us  [the longest x1 24.4 us: finish(): pl.pallas_call(finish_kernel, grid=(chunks + 1,), in_specs=[SM, SM, SM, S...]
    all_to_all x2 -> x1, waiting for transfers between devices: 7.02 us -> 4.69 us  [per_device(): lax.all_to_all(outgoing.reshape(count, CHUNK, PAN), axes, split_axis=0, c...]
    ppermute x0 -> x3, waiting for transfers between devices: none -> 2.24 us  [per_device(): lax.ppermute(piece, 'sub', [(i, (i + s) % subs) for i in range(subs)])]
    all_to_all x2 -> x1, starting transfers between devices: 14.1 us -> 11.9 us  [per_device(): lax.all_to_all(outgoing.reshape(count, CHUNK, PAN), axes, split_axis=0, c...]
    unnamed x26 -> x12, local copies, waits for them, and re-layouts: 2.96 us -> 1.55 us
    reshape x5 -> x0, local copies, waits for them, and re-layouts: 1.29 us -> none  [the longest x1 0.97 us: per_device(): ids = jnp.concatenate([far_ids, own_ids], 1).reshape(count * SLOT, 1)]
    pallas_call x1, Pallas kernels: 16.1 us -> 14.9 us  [near(): pl.pallas_call(near_kernel, grid=(1,), in_specs=[SM, SM] + [whole(x) for...]
  transfers between devices with their start and end apart: 4 -> 6, of which waited for: 2 -> 4; matrix products, arithmetic and copies ran while one was open for 3% -> 0% of each run, Pallas kernels for 23% -> 20%
where the time goes in v2:
time: 77 us; the launch traced here: 76.4 us
  Pallas kernels  44.9 us (58%)
  starting transfers between devices  22.9 us (30%)
  waiting for transfers between devices  6.93 us (9%)
  local copies, waits for them, and re-layouts  1.55 us (2%)
    pallas_call x1, Pallas kernels, finish(): pl.pallas_call(finish_kernel, grid=(chunks + 1,), in_specs=[SM, SM, SM, S...  24.4 us
    pallas_call x1, Pallas kernels, near(): pl.pallas_call(near_kernel, grid=(1,), in_specs=[SM, SM] + [whole(x) for...  14.9 us
    all_to_all x1, starting transfers between devices, per_device(): lax.all_to_all(outgoing.reshape(count, CHUNK, PAN), axes, split_axis=0, c...  11.9 us
    all_to_all x1, waiting for transfers between devices, per_device(): lax.all_to_all(outgoing.reshape(count, CHUNK, PAN), axes, split_axis=0, c...  4.69 us
    ppermute x1, starting transfers between devices, per_device(): low = lax.ppermute(low, axes, forward)  3.93 us
    ppermute x1, starting transfers between devices, per_device(): high = lax.ppermute(high, axes, backward)  3.75 us
    ppermute x3, starting transfers between devices, per_device(): lax.ppermute(piece, 'sub', [(i, (i + s) % subs) for i in range(subs)])  3.3 us
    pallas_call x1, Pallas kernels, upward(): pl.pallas_call(upward_kernel, grid=(1,), in_specs=[SM, SM] + [whole(x) fo...  3.24 us
  transfers between devices with their start and end apart: 6, of which 4 were waited for; matrix products, arithmetic and copies ran while one was open for 0% of the time, Pallas kernels for 20%

profile of v2, /device:TPU:1, one launch (start us, length us, event | category | flops | bytes accessed | tf_op | source)
XLA Modules:
  0.0 76.4 jit_solution(8652502880666582251)
XLA Ops:
  0.0 3.2 %upward.1 = (bf16[64,152]{1,0:T(8,128)(2,1)}, f32[16,152]{1,0:T(8,128)}, f32[16,152]{1,0:T(8,128)}, f32[16,152]{1,0:T(8,128)}, f32[16,152]{1,0:T(8,128)}, /*index=5*/f32[40,128]{1,0:T(8,128)}, f32[40,128]{1,0:T(8,128)}) custom-call(s32[1,16]{1,0:T(1,128)} %par.3, s32[1,16]{1,0:T(1,128)} %octs.3, f32[64,128]{1,0:T(8,128)} %bitcast.14, f32[3,16,128]{2,1,0:T(8,128)} %cen.3, ...), custom_call_target="tpu_custom_call" | custom-call | tf_op jit(solution)/shard_map/upward/pallas_call | solution.py:82
  3.2 3.9 %collective-permute-start.3 = (f32[40,128]{1,0:T(8,128)}, f32[40,128]{1,0:T(8,128)S(1)}, u32[]{:S(2)}, u32[]{:S(2)}) collective-permute-start(f32[40,128]{1,0:T(8,128)} %get-tuple-element.17), channel_id=1, source_target_pairs={{0,1},{1,2},{2,3},{3,4},{4,5},{5,6},{6,7},{7,8},{8,9},{9,10},{10,1... | collective-permute-start | bytes 61448 | tf_op jit(solution)/shard_map/ppermute | solution.py:511
  7.2 3.7 %collective-permute-start.4 = (f32[40,128]{1,0:T(8,128)}, f32[40,128]{1,0:T(8,128)S(1)}, u32[]{:S(2)}, u32[]{:S(2)}) collective-permute-start(f32[40,128]{1,0:T(8,128)} %get-tuple-element.18), channel_id=1, source_target_pairs={{1,0},{2,1},{3,2},{4,3},{5,4},{6,5},{7,6},{8,7},{9,8},{10,9},{11,1... | collective-permute-start | bytes 61448 | tf_op jit(solution)/shard_map/ppermute | solution.py:512
  10.9 0.1 collective-permute-start
  11.0 2.4 %collective-permute-start.1 = (f32[16,152]{1,0:T(8,128)}, f32[16,152]{1,0:T(8,128)S(1)}, u32[]{:S(2)}, u32[]{:S(2)}) collective-permute-start(f32[16,152]{1,0:T(8,128)} %get-tuple-element.15), channel_id=1, source_target_pairs={{0,2},{1,3},{2,0},{3,1},{4,6},{5,7},{6,4},{7,5},{8,10},{9,11},{10,... | collective-permute-start | bytes 29192 | tf_op jit(solution)/shard_map/ppermute | solution.py:505
  13.4 0.8 %collective-permute-start.2 = (f32[16,152]{1,0:T(8,128)}, f32[16,152]{1,0:T(8,128)S(1)}, u32[]{:S(2)}, u32[]{:S(2)}) collective-permute-start(f32[16,152]{1,0:T(8,128)} %get-tuple-element.16), channel_id=1, source_target_pairs={{0,3},{1,0},{2,1},{3,2},{4,7},{5,4},{6,5},{7,6},{8,11},{9,8},{10,9... | collective-permute-start | bytes 29192 | tf_op jit(solution)/shard_map/ppermute | solution.py:505
  14.3 0.8 %collective-permute-done.c1 = f32[16,152]{1,0:T(8,128)S(1)} collective-permute-done((f32[16,152]{1,0:T(8,128)}, f32[16,152]{1,0:T(8,128)S(1)}, u32[]{:S(2)}, u32[]{:S(2)}) %collective-permute-start) | collective-permute-done | bytes 9760 | tf_op jit(solution)/shard_map/ppermute | solution.py:505
  15.0 0.0 copy-start.3
  15.0 0.4 collective-permute-done.1.c2
  15.4 0.0 copy-start.4
  15.4 1.1 %collective-permute-done.2.c3 = f32[16,152]{1,0:T(8,128)S(1)} collective-permute-done((f32[16,152]{1,0:T(8,128)}, f32[16,152]{1,0:T(8,128)S(1)}, u32[]{:S(2)}, u32[]{:S(2)}) %collective-permute-start.2) | collective-permute-done | bytes 9760 | tf_op jit(solution)/shard_map/ppermute | solution.py:505
  16.5 0.0 copy-start.5
  16.5 0.0 collective-permute-done.3.low
  16.5 0.0 copy-start.1
  16.5 0.0 collective-permute-done.4.high
  16.5 0.0 copy-start.2
  16.5 0.0 copy-done.3
  16.5 0.0 copy-done.4
  16.5 0.6 copy-done.5
  17.1 0.0 copy-done.1
  17.1 0.0 copy-done.2
  17.1 2.3 %pack.1 = bf16[4096,128]{1,0:T(8,128)(2,1)} custom-call(s32[2,128]{1,0:T(2,128)} %bitcast.16, s32[1,128]{1,0:T(1,128)} %counts.1, bf16[64,152]{1,0:T(8,128)(2,1)} %get-tuple-element.12.mult, f32[16,152]{1,0:T(8,128)} %get-tuple-element.13.c0, f32[16,152]{1,0:T(8,128)} %copy-done.3, f32[16,152]{1,0:T(8,128)} %copy-done.4, f32[16,152]{1,0:T(8,128)} %copy-done.5, ...), custom_call_target="tpu_custom_call" | custom-call | tf_op jit(solution)/shard_map/pack/pallas_call | solution.py:129
  19.4 11.9 %all-to-all-start = ((bf16[128,32,128]{2,1,0:T(8,128)(2,1)}), bf16[128,32,128]{2,1,0:T(8,128)(2,1)S(1)}, u32[]{:S(2)}, u32[]{:S(2)}) async-start(bf16[128,32,128]{2,1,0:T(8,128)(2,1)} %bitcast.12), calls=%async_computation | async-start | bytes 2097152 | tf_op jit(solution)/shard_map/all_to_all | solution.py:515
  31.4 14.9 %near.1.near_part = f32[64,128]{1,0:T(8,128)} custom-call(s32[16,27]{1,0:T(8,128)} %index.1, s32[16]{0:T(128)} %count.1, f32[3,16,128]{2,1,0:T(8,128)} %cen.3, f32[3,16,128]{2,1,0:T(8,128)} %nrm.3, f32[64,128]{1,0:T(8,128)} %bitcast.15, f32[40,128]{1,0:T(8,128)} %copy-done.1, f32[40,128]{1,0:T(8,128)} %copy-done.2), custom_call_target="tpu_custom_call" | custom-call | flops 2000000000 | bytes 1000000 | tf_op jit(solution)/shard_map/near/pallas_call | solution.py:253
  46.3 4.7 %all-to-all-done = bf16[128,32,128]{2,1,0:T(8,128)(2,1)S(1)} async-done(((bf16[128,32,128]{2,1,0:T(8,128)(2,1)}), bf16[128,32,128]{2,1,0:T(8,128)(2,1)S(1)}, u32[]{:S(2)}, u32[]{:S(2)}) %all-to-all-start) | async-done | bytes 1048608 | tf_op jit(solution)/shard_map/all_to_all | solution.py:515
  51.0 0.0 copy-start
  51.0 1.0 %copy-done = bf16[128,32,128]{2,1,0:T(8,128)(2,1)} copy-done((bf16[128,32,128]{2,1,0:T(8,128)(2,1)}, bf16[128,32,128]{2,1,0:T(8,128)(2,1)S(1)}, u32[]{:S(2)}) %copy-start) | copy-done | bytes 1048600
  51.9 24.4 %finish.1 = f32[64,128]{1,0:T(8,128)} custom-call(s32[1,16]{1,0:T(1,128)} %par.3, s32[1,16]{1,0:T(1,128)} %octs.3, s32[16]{0:T(128)} %far_count.1, s32[16]{0:T(128)} %top_count.1, s32[16,64]{1,0:T(8,128)} %far_slot.1, s32[16,64]{1,0:T(8,128)} %far_op.1, s32[16,32]{1,0:T(8,128)} %top_src.1, s32[16,32]{1,0:T(8,128)} %top_op.1, bf16[4096,128]{1,0:T(8,128)(2,1)} %bitcast.11, ...), custom_call_target="tpu_custom_call" | custom-call | tf_op jit(solution)/shard_map/finish/pallas_call | solution.py:433
Async XLA Ops:
  3.2 13.3 %collective-permute-start.3 = (f32[40,128]{1,0:T(8,128)}, f32[40,128]{1,0:T(8,128)S(1)}, u32[]{:S(2)}, u32[]{:S(2)}) collective-permute-start(f32[40,128]{1,0:T(8,128)} %get-tuple-element.17), channel_id=1, source_target_pairs={{0,1},{1,2},{2,3},{3,4},{4,5},{5,6},{6,7},{7,8},{8,9},{9,10},{10,1... | collective-permute-start | bytes 61448 | tf_op jit(solution)/shard_map/ppermute | solution.py:511
  7.2 9.3 %collective-permute-start.4 = (f32[40,128]{1,0:T(8,128)}, f32[40,128]{1,0:T(8,128)S(1)}, u32[]{:S(2)}, u32[]{:S(2)}) collective-permute-start(f32[40,128]{1,0:T(8,128)} %get-tuple-element.18), channel_id=1, source_target_pairs={{1,0},{2,1},{3,2},{4,3},{5,4},{6,5},{7,6},{8,7},{9,8},{10,9},{11,1... | collective-permute-start | bytes 61448 | tf_op jit(solution)/shard_map/ppermute | solution.py:512
  10.9 4.1 %collective-permute-start = (f32[16,152]{1,0:T(8,128)}, f32[16,152]{1,0:T(8,128)S(1)}, u32[]{:S(2)}, u32[]{:S(2)}) collective-permute-start(f32[16,152]{1,0:T(8,128)} %get-tuple-element.14), channel_id=1, source_target_pairs={{0,1},{1,2},{2,3},{3,0},{4,5},{5,6},{6,7},{7,4},{8,9},{9,10},{10,1... | collective-permute-start | bytes 29192 | tf_op jit(solution)/shard_map/ppermute | solution.py:505
  11.0 4.4 %collective-permute-start.1 = (f32[16,152]{1,0:T(8,128)}, f32[16,152]{1,0:T(8,128)S(1)}, u32[]{:S(2)}, u32[]{:S(2)}) collective-permute-start(f32[16,152]{1,0:T(8,128)} %get-tuple-element.15), channel_id=1, source_target_pairs={{0,2},{1,3},{2,0},{3,1},{4,6},{5,7},{6,4},{7,5},{8,10},{9,11},{10,... | collective-permute-start | bytes 29192 | tf_op jit(solution)/shard_map/ppermute | solution.py:505
  13.4 3.1 %collective-permute-start.2 = (f32[16,152]{1,0:T(8,128)}, f32[16,152]{1,0:T(8,128)S(1)}, u32[]{:S(2)}, u32[]{:S(2)}) collective-permute-start(f32[16,152]{1,0:T(8,128)} %get-tuple-element.16), channel_id=1, source_target_pairs={{0,3},{1,0},{2,1},{3,2},{4,7},{5,4},{6,5},{7,6},{8,11},{9,8},{10,9... | collective-permute-start | bytes 29192 | tf_op jit(solution)/shard_map/ppermute | solution.py:505
  15.0 1.5 %copy-start.3 = (f32[16,152]{1,0:T(8,128)}, f32[16,152]{1,0:T(8,128)S(1)}, u32[]{:S(2)}) copy-start(f32[16,152]{1,0:T(8,128)S(1)} %collective-permute-done.c1) | copy-start | bytes 29188
  15.4 1.1 %copy-start.4 = (f32[16,152]{1,0:T(8,128)}, f32[16,152]{1,0:T(8,128)S(1)}, u32[]{:S(2)}) copy-start(f32[16,152]{1,0:T(8,128)S(1)} %collective-permute-done.1.c2) | copy-start | bytes 29188
  16.5 0.6 copy-start.5
  16.5 0.6 copy-start.1
  16.5 0.6 copy-start.2
  19.4 31.5 %all-to-all-start = ((bf16[128,32,128]{2,1,0:T(8,128)(2,1)}), bf16[128,32,128]{2,1,0:T(8,128)(2,1)S(1)}, u32[]{:S(2)}, u32[]{:S(2)}) async-start(bf16[128,32,128]{2,1,0:T(8,128)(2,1)} %bitcast.12), calls=%async_computation | async-start | bytes 2097152 | tf_op jit(solution)/shard_map/all_to_all | solution.py:515
  51.0 1.0 %copy-start = (bf16[128,32,128]{2,1,0:T(8,128)(2,1)}, bf16[128,32,128]{2,1,0:T(8,128)(2,1)S(1)}, u32[]{:S(2)}) copy-start(bf16[128,32,128]{2,1,0:T(8,128)(2,1)S(1)} %all-to-all-done) | copy-start | bytes 3145732

commit v3 on v2

--- a/solution.py
+++ b/solution.py
@@ -44,7 +44,7 @@
     return lax.broadcasted_iota(i32, shape, dim)
 
 
-def upward_kernel(par, octs, dens, cen, nrm, tm, m2m, mult_out, c0, c1, c2, c3, low_out, high_out):
+def upward_kernel(par, octs, dens, cen, nrm, tm, m2m, mult_out, c0, x1, c2, x3, cross):
     d = dens[...].astype(bf16)
     leaf_row = iota((ROWS, EQ), 0) % LEAF
     mult = jnp.zeros((ROWS, EQ), f32)
@@ -63,22 +63,35 @@
     box = ((row // 16 + lax.axis_index("sub")) % 4) * 4 + row % 4
     hit = (parent == box) & ((row // 4) % 4 == lane // LEAF)
     part = nn(hit.astype(f32), child, precision=lax.Precision.HIGHEST)
-    for s, piece in enumerate((c0, c1, c2, c3)):
-        piece[...] = part[16 * s : 16 * s + 16]
+    for s, piece in enumerate((c0, x1, c2, x3)):
+        piece[:16, :] = part[16 * s : 16 * s + 16]
+    first = lax.axis_index("sub") == 0
+
+    def rim(at, ends, starts):
+        x1[16 + at : 16 + at + RIM, :PAN] = ends
+        x3[16 + at : 16 + at + RIM, :PAN] = starts
+        cross[at : at + RIM, :] = jnp.where(first, starts, ends)
+
     for a in range(3):
-        high_out[4 * a : 4 * a + 4, :] = cen[a, :RIM, :]
-        low_out[4 * a : 4 * a + 4, :] = cen[a, LEAF - RIM :, :]
-        high_out[12 + 4 * a : 16 + 4 * a, :] = nrm[a, :RIM, :]
-        low_out[12 + 4 * a : 16 + 4 * a, :] = nrm[a, LEAF - RIM :, :]
+        rim(RIM * a, cen[a, LEAF - RIM :, :], cen[a, :RIM, :])
+        rim(RIM * (3 + a), nrm[a, LEAF - RIM :, :], nrm[a, :RIM, :])
     for r in range(RHS):
-        high_out[24 + 4 * r : 28 + 4 * r, :] = dens[LEAF * r : LEAF * r + RIM, :]
-        low_out[24 + 4 * r : 28 + 4 * r, :] = dens[LEAF * (r + 1) - RIM : LEAF * (r + 1), :]
+        rim(
+            RIM * (6 + r),
+            dens[LEAF * (r + 1) - RIM : LEAF * (r + 1), :],
+            dens[LEAF * r : LEAF * r + RIM, :],
+        )
+    for x in (x1, x3):
+        x[16:, PAN:] = jnp.zeros((40, EQ - PAN), f32)
+
+
 def upward(par, octs, dens, cen, nrm, tm, m2m):
     outs = [
         jax.ShapeDtypeStruct((ROWS, EQ), bf16),
     ]
-    outs += [jax.ShapeDtypeStruct((16, EQ), f32)] * 4
-    outs += [jax.ShapeDtypeStruct((40, PAN), f32)] * 2
+    small = jax.ShapeDtypeStruct((16, EQ), f32)
+    large = jax.ShapeDtypeStruct((56, EQ), f32)
+    outs += [small, large, small, large, jax.ShapeDtypeStruct((40, PAN), f32)]
     return pl.pallas_call(
         upward_kernel,
         grid=(1,),
@@ -90,10 +103,10 @@
     )(par, octs, dens, cen, nrm, tm, m2m)
 
 
-def pack_kernel(boxes, counts, mult, c0, c1, c2, c3, low, high, out, far, const):
+def pack_kernel(boxes, counts, mult, c0, x1, c2, x3, cross, out, far, const):
     row = iota((EQ, BOX), 0)
     lane = iota((EQ, BOX), 1)
-    own = (c0[...] + c1[...]) + (c2[...] + c3[...])
+    own = (c0[...] + x1[:16, :]) + (c2[...] + x3[:16, :])
     own = own.astype(bf16).astype(f32)
     mf = mult[...].astype(f32)
     table = jnp.zeros((24, BOX), f32)
@@ -152,10 +165,14 @@
     return a, b, c
 
 
-def near_kernel(index, count, cen, nrm, dens, low, high, out, raw, fsrc, ftar, fs, dpar, dwide, ft, sums, dist):
+def near_kernel(index, count, cen, nrm, dens, x1, x3, cross, out, raw, fsrc, ftar, fs, dpar, dwide, ft, sums, dist):
+    place = lax.axis_index("sub")
+    last = lax.axis_size("sub") - 1
     for q in range(10):
-        raw[q, 0:RIM, :] = low[4 * q : 4 * q + 4, :]
-        raw[q, RIM + LEAF : SRC, :] = high[4 * q : 4 * q + 4, :]
+        far_side = cross[4 * q : 4 * q + 4, :]
+        at = 16 + 4 * q
+        raw[q, 0:RIM, :] = jnp.where(place == 0, far_side, x1[at : at + RIM, :PAN])
+        raw[q, RIM + LEAF : SRC, :] = jnp.where(place == last, far_side, x3[at : at + RIM, :PAN])
         if q < 3:
             body = cen[q]
         elif q < 6:
@@ -248,12 +265,12 @@
         out[LEAF * r : LEAF * (r + 1), :] = jnp.sum(sums[:, r], 1)
 
 
-def near(index, count, cen, nrm, dens, low, high):
+def near(index, count, cen, nrm, dens, x1, x3, cross):
     outs = jax.ShapeDtypeStruct((ROWS, PAN), f32)
     return pl.pallas_call(
         near_kernel,
         grid=(1,),
-        in_specs=[SM, SM] + [whole(x) for x in (cen, nrm, dens, low, high)],
+        in_specs=[SM, SM] + [whole(x) for x in (cen, nrm, dens, x1, x3, cross)],
         out_specs=whole(outs),
         out_shape=outs,
         scratch_shapes=[
@@ -272,21 +289,27 @@
             flops=20_000_000_00, bytes_accessed=1_000_000, transcendentals=3_600_000
         ),
         name="near",
-    )(index, count, cen, nrm, dens, low, high)
+    )(index, count, cen, nrm, dens, x1, x3, cross)
 
 
 def finish_kernel(
-    par, octs, far_count, top_count, far_slot, far_op, top_src, top_op, arrived, ops0, ops1, l2l, tp, near_part, out,
-    ids, slots, kinds, turned, picked, s0, s1, s2, m0, m1, m2, m3, m4, m5, acc,
+    par, octs, far_count, top_count, far_slot, far_op, top_src, top_op, arrived, ops0, ops1, l2l_hbm, tp_hbm, near_part, out,
+    ids, slots, kinds, turned, picked, s0, s1, s2, m0, m1, m2, m3, m4, m5, acc, l2l, tp, sems,
 ):
     step = pl.program_id(0)
     spread = (s0, s1, s2)
+    late = (
+        pltpu.make_async_copy(l2l_hbm, l2l, sems.at[0]),
+        pltpu.make_async_copy(tp_hbm, tp, sems.at[1]),
+    )
     even = (m0, m1, m2)
     odd = (m3, m4, m5)
     tail = ops0.shape[2] - 2 * PAN
 
     @pl.when(step == 0)
     def _():
+        for copy in late:
+            copy.start()
         acc[...] = jnp.zeros_like(acc)
         m2[...] = jnp.zeros_like(m2)
         m5[...] = jnp.zeros_like(m5)
@@ -405,6 +428,8 @@
     @pl.when(step == last)
     def _():
         multiply(EQ % FB, odd)
+        for copy in late:
+            copy.wait()
         res = acc[...].T
         far = res[:ROWS]
         top = res[ROWS:].astype(bf16)
@@ -445,8 +470,8 @@
             whole(arrived),
             pl.BlockSpec(half, lambda i: (0, jnp.minimum(i, chunks - 1), 0)),
             pl.BlockSpec(half, lambda i: (1, jnp.minimum(i, chunks - 1), 0)),
-            whole(l2l),
-            whole(tp),
+            pl.BlockSpec(memory_space=pl.ANY),
+            pl.BlockSpec(memory_space=pl.ANY),
             whole(near_part),
         ],
         out_specs=pl.BlockSpec((ROWS, PAN), lambda i: (0, 0)),
@@ -467,6 +492,9 @@
             pltpu.VMEM((EQ * FB, PAN), f32),
             pltpu.VMEM((EQ * FB, PAN), f32),
             pltpu.VMEM((EQ, 2 * ROWS), f32),
+            pltpu.VMEM(l2l.shape, bf16),
+            pltpu.VMEM(tp.shape, bf16),
+            pltpu.SemaphoreType.DMA((2,)),
         ],
         compiler_params=pltpu.CompilerParams(vmem_limit_bytes=BIG),
         name="finish",
@@ -496,27 +524,24 @@
     top_count,
 ):
     dens = density.reshape(ROWS, PAN)
-    mult, own, *others, low, high = upward(
+    mult, own, *others, cross = upward(
         parent_of, octant, dens, centres, normal, to_multipole, m2m_ops
     )
+    axes = ("leaf", "sub")
     subs = lax.axis_size("sub")
+    count = lax.axis_size("leaf") * subs
     pieces = [own]
     for s, piece in enumerate(others, 1):
         pieces.append(lax.ppermute(piece, "sub", [(i, (i + s) % subs) for i in range(subs)]))
-
-    axes = ("leaf", "sub")
-    count = lax.axis_size("leaf") * lax.axis_size("sub")
-    forward = [(i, i + 1) for i in range(count - 1)]
-    backward = [(i + 1, i) for i in range(count - 1)]
-    low = lax.ppermute(low, axes, forward)
-    high = lax.ppermute(high, axes, backward)
-
-    outgoing = pack(jnp.transpose(send_box[0]), send_count, mult, pieces, (low, high))
+    ends = range(subs - 1, count - 1, subs)
+    cross = lax.ppermute(cross, axes, [(i, i + 1) for i in ends] + [(i + 1, i) for i in ends])
+
+    outgoing = pack(jnp.transpose(send_box[0]), send_count, mult, pieces, (cross,))
     arrived = lax.all_to_all(
         outgoing.reshape(count, CHUNK, PAN), axes, split_axis=0, concat_axis=0, tiled=True
     )
 
-    near_part = near(near_index, near_count, centres, normal, dens, low, high)
+    near_part = near(near_index, near_count, centres, normal, dens, pieces[1], pieces[3], cross)
 
     res = finish(
         parent_of,

time: 77 us -> 73.1 us (0.949)
  starting transfers between devices: 22.9 us -> 17.4 us
  waiting for transfers between devices: 6.93 us -> 8.18 us
    ppermute x2 -> x1, starting transfers between devices: 7.68 us -> 4.41 us  [per_device(): lax.ppermute(cross, axes, [(i, i + 1) for i in ends] + [(i + 1, i) for i...]
    all_to_all x1, starting transfers between devices: 11.9 us -> 9.49 us  [per_device(): lax.all_to_all(outgoing.reshape(count, CHUNK, PAN), axes, split_axis=0, c...]
    ppermute x3, waiting for transfers between devices: 2.24 us -> 4.3 us  [per_device(): lax.ppermute(piece, 'sub', [(i, (i + s) % subs) for i in range(subs)])]
    pallas_call x1, Pallas kernels: 14.9 us -> 15.7 us  [near(): pl.pallas_call(near_kernel, grid=(1,), in_specs=[SM, SM] + [whole(x) for...]
    all_to_all x1, waiting for transfers between devices: 4.69 us -> 3.88 us  [per_device(): lax.all_to_all(outgoing.reshape(count, CHUNK, PAN), axes, split_axis=0, c...]
    unnamed x12 -> x10, local copies, waits for them, and re-layouts: 1.55 us -> 1.59 us
  transfers between devices with their start and end apart: 6 -> 5, of which waited for: 4 -> 2; matrix products, arithmetic and copies ran while one was open for 0% -> 0% of each run, Pallas kernels for 20% -> 22%
where the time goes in v3:
time: 73.1 us; the launch traced here: 72.6 us
  Pallas kernels  45.4 us (62%)
  starting transfers between devices  17.4 us (24%)
  waiting for transfers between devices  8.18 us (11%)
  local copies, waits for them, and re-layouts  1.59 us (2%)
    pallas_call x1, Pallas kernels, finish(): pl.pallas_call(finish_kernel, grid=(chunks + 1,), in_specs=[SM, SM, SM, S...  24 us
    pallas_call x1, Pallas kernels, near(): pl.pallas_call(near_kernel, grid=(1,), in_specs=[SM, SM] + [whole(x) for...  15.7 us
    all_to_all x1, starting transfers between devices, per_device(): lax.all_to_all(outgoing.reshape(count, CHUNK, PAN), axes, split_axis=0, c...  9.49 us
    ppermute x1, starting transfers between devices, per_device(): lax.ppermute(cross, axes, [(i, i + 1) for i in ends] + [(i + 1, i) for i...  4.41 us
    ppermute x3, waiting for transfers between devices, per_device(): lax.ppermute(piece, 'sub', [(i, (i + s) % subs) for i in range(subs)])  4.3 us
    all_to_all x1, waiting for transfers between devices, per_device(): lax.all_to_all(outgoing.reshape(count, CHUNK, PAN), axes, split_axis=0, c...  3.88 us
    ppermute x3, starting transfers between devices, per_device(): lax.ppermute(piece, 'sub', [(i, (i + s) % subs) for i in range(subs)])  3.46 us
    pallas_call x1, Pallas kernels, upward(): pl.pallas_call(upward_kernel, grid=(1,), in_specs=[SM, SM] + [whole(x) fo...  3.27 us
  transfers between devices with their start and end apart: 5, of which 2 were waited for; matrix products, arithmetic and copies ran while one was open for 0% of the time, Pallas kernels for 22%

profile of v3, /device:TPU:1, one launch (start us, length us, event | category | flops | bytes accessed | tf_op | source)
XLA Modules:
  0.0 72.6 jit_solution(11235137498989218479)
XLA Ops:
  0.0 3.3 %upward.1 = (bf16[64,152]{1,0:T(8,128)(2,1)}, f32[16,152]{1,0:T(8,128)}, f32[56,152]{1,0:T(8,128)}, f32[16,152]{1,0:T(8,128)}, f32[56,152]{1,0:T(8,128)}, /*index=5*/f32[40,128]{1,0:T(8,128)}) custom-call(s32[1,16]{1,0:T(1,128)} %par.3, s32[1,16]{1,0:T(1,128)} %octs.3, f32[64,128]{1,0:T(8,128)} %bitcast.14, f32[3,16,128]{2,1,0:T(8,128)} %cen.3, ...), custom_call_target="tpu_custom_call" | custom-call | tf_op jit(solution)/shard_map/upward/pallas_call | solution.py:95
  3.3 2.0 %collective-permute-start = (f32[56,152]{1,0:T(8,128)}, f32[56,152]{1,0:T(8,128)S(1)}, u32[]{:S(2)}, u32[]{:S(2)}) collective-permute-start(f32[56,152]{1,0:T(8,128)} %get-tuple-element.13), channel_id=1, source_target_pairs={{0,1},{1,2},{2,3},{3,0},{4,5},{5,6},{6,7},{7,4},{8,9},{9,10},{10,1... | collective-permute-start | bytes 102152 | tf_op jit(solution)/shard_map/ppermute | solution.py:535
  5.3 1.3 %collective-permute-start.2 = (f32[56,152]{1,0:T(8,128)}, f32[56,152]{1,0:T(8,128)S(1)}, u32[]{:S(2)}, u32[]{:S(2)}) collective-permute-start(f32[56,152]{1,0:T(8,128)} %get-tuple-element.15), channel_id=1, source_target_pairs={{0,3},{1,0},{2,1},{3,2},{4,7},{5,4},{6,5},{7,6},{8,11},{9,8},{10,9... | collective-permute-start | bytes 102152 | tf_op jit(solution)/shard_map/ppermute | solution.py:535
  6.7 4.4 %collective-permute-start.3 = (f32[40,128]{1,0:T(8,128)}, f32[40,128]{1,0:T(8,128)S(1)}, u32[]{:S(2)}, u32[]{:S(2)}) collective-permute-start(f32[40,128]{1,0:T(8,128)} %get-tuple-element.16), channel_id=1, source_target_pairs={{3,4},{7,8},{11,12},{15,16},{19,20},{23,24},{27,28},{31,32},{35,36... | collective-permute-start | bytes 61448 | tf_op jit(solution)/shard_map/ppermute | solution.py:537
  11.1 0.1 collective-permute-start.1
  11.2 4.3 %collective-permute-done.1.c2 = f32[16,152]{1,0:T(8,128)S(1)} collective-permute-done((f32[16,152]{1,0:T(8,128)}, f32[16,152]{1,0:T(8,128)S(1)}, u32[]{:S(2)}, u32[]{:S(2)}) %collective-permute-start.1) | collective-permute-done | bytes 9760 | tf_op jit(solution)/shard_map/ppermute | solution.py:535
  15.5 0.0 copy-start.4
  15.5 0.0 collective-permute-done.3.cross
  15.5 0.0 copy-start.3
  15.5 0.0 collective-permute-done.x1
  15.5 0.0 copy-start.1
  15.5 0.0 collective-permute-done.2.x3
  15.5 0.0 copy-start.2
  15.5 0.6 copy-done.4
  16.0 0.0 copy-done.3
  16.1 0.0 copy-done.1
  16.1 0.0 copy-done.2
  16.1 2.4 %pack.1 = bf16[4096,128]{1,0:T(8,128)(2,1)} custom-call(s32[2,128]{1,0:T(2,128)} %bitcast.16, s32[1,128]{1,0:T(1,128)} %counts.1, bf16[64,152]{1,0:T(8,128)(2,1)} %get-tuple-element.11.mult, f32[16,152]{1,0:T(8,128)} %get-tuple-element.12.c0, f32[56,152]{1,0:T(8,128)} %copy-done.1, f32[16,152]{1,0:T(8,128)} %copy-done.4, f32[56,152]{1,0:T(8,128)} %copy-done.2, ...), custom_call_target="tpu_custom_call" | custom-call | tf_op jit(solution)/shard_map/pack/pallas_call | solution.py:142
  18.5 9.5 %all-to-all-start = ((bf16[128,32,128]{2,1,0:T(8,128)(2,1)}), bf16[128,32,128]{2,1,0:T(8,128)(2,1)S(1)}, u32[]{:S(2)}, u32[]{:S(2)}) async-start(bf16[128,32,128]{2,1,0:T(8,128)(2,1)} %bitcast.12), calls=%async_computation | async-start | bytes 2097152 | tf_op jit(solution)/shard_map/all_to_all | solution.py:540
  28.0 15.7 %near.1.near_part = f32[64,128]{1,0:T(8,128)} custom-call(s32[16,27]{1,0:T(8,128)} %index.1, s32[16]{0:T(128)} %count.1, f32[3,16,128]{2,1,0:T(8,128)} %cen.3, f32[3,16,128]{2,1,0:T(8,128)} %nrm.3, f32[64,128]{1,0:T(8,128)} %bitcast.15, f32[56,152]{1,0:T(8,128)} %copy-done.1, f32[56,152]{1,0:T(8,128)} %copy-done.2, f32[40,128]{1,0:T(8,128)} %copy-done.3), custom_call_target="tpu_custom_call" | custom-call | flops 2000000000 | bytes 1000000 | tf_op jit(solution)/shard_map/near/pallas_call | solution.py:270
  43.7 3.9 %all-to-all-done = bf16[128,32,128]{2,1,0:T(8,128)(2,1)S(1)} async-done(((bf16[128,32,128]{2,1,0:T(8,128)(2,1)}), bf16[128,32,128]{2,1,0:T(8,128)(2,1)S(1)}, u32[]{:S(2)}, u32[]{:S(2)}) %all-to-all-start) | async-done | bytes 1048608 | tf_op jit(solution)/shard_map/all_to_all | solution.py:540
  47.6 0.0 copy-start
  47.6 1.0 %copy-done = bf16[128,32,128]{2,1,0:T(8,128)(2,1)} copy-done((bf16[128,32,128]{2,1,0:T(8,128)(2,1)}, bf16[128,32,128]{2,1,0:T(8,128)(2,1)S(1)}, u32[]{:S(2)}) %copy-start) | copy-done | bytes 1048600
  48.6 24.0 %finish.1 = f32[64,128]{1,0:T(8,128)} custom-call(s32[1,16]{1,0:T(1,128)} %par.3, s32[1,16]{1,0:T(1,128)} %octs.3, s32[16]{0:T(128)} %far_count.1, s32[16]{0:T(128)} %top_count.1, s32[16,64]{1,0:T(8,128)} %far_slot.1, s32[16,64]{1,0:T(8,128)} %far_op.1, s32[16,32]{1,0:T(8,128)} %top_src.1, s32[16,32]{1,0:T(8,128)} %top_op.1, bf16[4096,128]{1,0:T(8,128)(2,1)} %bitcast.11, ...), custom_call_target="tpu_custom_call" | custom-call | tf_op jit(solution)/shard_map/finish/pallas_call | solution.py:458
Async XLA Ops:
  3.3 12.2 %collective-permute-start = (f32[56,152]{1,0:T(8,128)}, f32[56,152]{1,0:T(8,128)S(1)}, u32[]{:S(2)}, u32[]{:S(2)}) collective-permute-start(f32[56,152]{1,0:T(8,128)} %get-tuple-element.13), channel_id=1, source_target_pairs={{0,1},{1,2},{2,3},{3,0},{4,5},{5,6},{6,7},{7,4},{8,9},{9,10},{10,1... | collective-permute-start | bytes 102152 | tf_op jit(solution)/shard_map/ppermute | solution.py:535
  5.3 10.2 %collective-permute-start.2 = (f32[56,152]{1,0:T(8,128)}, f32[56,152]{1,0:T(8,128)S(1)}, u32[]{:S(2)}, u32[]{:S(2)}) collective-permute-start(f32[56,152]{1,0:T(8,128)} %get-tuple-element.15), channel_id=1, source_target_pairs={{0,3},{1,0},{2,1},{3,2},{4,7},{5,4},{6,5},{7,6},{8,11},{9,8},{10,9... | collective-permute-start | bytes 102152 | tf_op jit(solution)/shard_map/ppermute | solution.py:535
  6.7 8.8 %collective-permute-start.3 = (f32[40,128]{1,0:T(8,128)}, f32[40,128]{1,0:T(8,128)S(1)}, u32[]{:S(2)}, u32[]{:S(2)}) collective-permute-start(f32[40,128]{1,0:T(8,128)} %get-tuple-element.16), channel_id=1, source_target_pairs={{3,4},{7,8},{11,12},{15,16},{19,20},{23,24},{27,28},{31,32},{35,36... | collective-permute-start | bytes 61448 | tf_op jit(solution)/shard_map/ppermute | solution.py:537
  11.1 4.4 %collective-permute-start.1 = (f32[16,152]{1,0:T(8,128)}, f32[16,152]{1,0:T(8,128)S(1)}, u32[]{:S(2)}, u32[]{:S(2)}) collective-permute-start(f32[16,152]{1,0:T(8,128)} %get-tuple-element.14), channel_id=1, source_target_pairs={{0,2},{1,3},{2,0},{3,1},{4,6},{5,7},{6,4},{7,5},{8,10},{9,11},{10,... | collective-permute-start | bytes 29192 | tf_op jit(solution)/shard_map/ppermute | solution.py:535
  15.5 0.6 copy-start.4
  15.5 0.6 copy-start.3
  15.5 0.6 copy-start.1
  15.5 0.6 copy-start.2
  18.5 29.1 %all-to-all-start = ((bf16[128,32,128]{2,1,0:T(8,128)(2,1)}), bf16[128,32,128]{2,1,0:T(8,128)(2,1)S(1)}, u32[]{:S(2)}, u32[]{:S(2)}) async-start(bf16[128,32,128]{2,1,0:T(8,128)(2,1)} %bitcast.12), calls=%async_computation | async-start | bytes 2097152 | tf_op jit(solution)/shard_map/all_to_all | solution.py:540
  47.6 1.0 %copy-start = (bf16[128,32,128]{2,1,0:T(8,128)(2,1)}, bf16[128,32,128]{2,1,0:T(8,128)(2,1)S(1)}, u32[]{:S(2)}) copy-start(bf16[128,32,128]{2,1,0:T(8,128)(2,1)S(1)} %all-to-all-done) | copy-start | bytes 3145732

commit v4 on v3

--- a/solution.py
+++ b/solution.py
@@ -23,7 +23,7 @@
 EPS = 0.01
 FB = 16
 MIB = 1 << 20
-BIG = 56 * MIB
+BIG = 64 * MIB
 
 SM = pl.BlockSpec(memory_space=pltpu.SMEM)
 

time: 73.1 us -> 71.7 us (0.981)
  local copies, waits for them, and re-layouts: 1.59 us -> 0 us
  Pallas kernels: 45.4 us -> 43.9 us
  waiting for transfers between devices: 8.18 us -> 9.46 us
    unnamed x10 -> x0, local copies, waits for them, and re-layouts: 1.59 us -> none
    pallas_call x1, Pallas kernels: 15.7 us -> 14.2 us  [near(): pl.pallas_call(near_kernel, grid=(1,), in_specs=[SM, SM] + [whole(x) for...]
    all_to_all x1, waiting for transfers between devices: 3.88 us -> 5.05 us  [per_device(): lax.all_to_all(outgoing.reshape(count, CHUNK, PAN), axes, split_axis=0, c...]
  transfers between devices with their start and end apart: 5 -> 5, of which waited for: 2 -> 2; matrix products, arithmetic and copies ran while one was open for 0% -> 0% of each run, Pallas kernels for 22% -> 20%
where the time goes in v4:
time: 71.7 us; the launch traced here: 71.2 us
  Pallas kernels  43.9 us (61%)
  starting transfers between devices  17.8 us (25%)
  waiting for transfers between devices  9.46 us (13%)
    pallas_call x1, Pallas kernels, finish(): pl.pallas_call(finish_kernel, grid=(chunks + 1,), in_specs=[SM, SM, SM, S...  24 us
    pallas_call x1, Pallas kernels, near(): pl.pallas_call(near_kernel, grid=(1,), in_specs=[SM, SM] + [whole(x) for...  14.2 us
    all_to_all x1, starting transfers between devices, per_device(): lax.all_to_all(outgoing.reshape(count, CHUNK, PAN), axes, split_axis=0, c...  9.95 us
    all_to_all x1, waiting for transfers between devices, per_device(): lax.all_to_all(outgoing.reshape(count, CHUNK, PAN), axes, split_axis=0, c...  5.05 us
    ppermute x1, starting transfers between devices, per_device(): lax.ppermute(cross, axes, [(i, i + 1) for i in ends] + [(i + 1, i) for i...  4.41 us
    ppermute x3, waiting for transfers between devices, per_device(): lax.ppermute(piece, 'sub', [(i, (i + s) % subs) for i in range(subs)])  4.4 us
    ppermute x3, starting transfers between devices, per_device(): lax.ppermute(piece, 'sub', [(i, (i + s) % subs) for i in range(subs)])  3.47 us
    pallas_call x1, Pallas kernels, upward(): pl.pallas_call(upward_kernel, grid=(1,), in_specs=[SM, SM] + [whole(x) fo...  3.28 us
  transfers between devices with their start and end apart: 5, of which 2 were waited for; matrix products, arithmetic and copies ran while one was open for 0% of the time, Pallas kernels for 20%

profile of v4, /device:TPU:1, one launch (start us, length us, event | category | flops | bytes accessed | tf_op | source)
XLA Modules:
  0.0 71.2 jit_solution(13942253676860074560)
XLA Ops:
  0.0 3.3 %upward.1 = (bf16[64,152]{1,0:T(8,128)(2,1)}, f32[16,152]{1,0:T(8,128)}, f32[56,152]{1,0:T(8,128)}, f32[16,152]{1,0:T(8,128)}, f32[56,152]{1,0:T(8,128)}, /*index=5*/f32[40,128]{1,0:T(8,128)}) custom-call(s32[1,16]{1,0:T(1,128)} %par.3, s32[1,16]{1,0:T(1,128)} %octs.3, f32[64,128]{1,0:T(8,128)} %bitcast.13, f32[3,16,128]{2,1,0:T(8,128)} %cen.3, ...), custom_call_target="tpu_custom_call" | custom-call | tf_op jit(solution)/shard_map/upward/pallas_call | solution.py:95
  3.3 2.0 %collective-permute-start = (f32[56,152]{1,0:T(8,128)}, f32[56,152]{1,0:T(8,128)}, u32[]{:S(2)}, u32[]{:S(2)}) collective-permute-start(f32[56,152]{1,0:T(8,128)} %get-tuple-element.13), channel_id=1, source_target_pairs={{0,1},{1,2},{2,3},{3,0},{4,5},{5,6},{6,7},{7,4},{8,9},{9,10},{10,1... | collective-permute-start | bytes 102152 | tf_op jit(solution)/shard_map/ppermute | solution.py:535
  5.3 1.3 %collective-permute-start.2 = (f32[56,152]{1,0:T(8,128)}, f32[56,152]{1,0:T(8,128)}, u32[]{:S(2)}, u32[]{:S(2)}) collective-permute-start(f32[56,152]{1,0:T(8,128)} %get-tuple-element.15), channel_id=1, source_target_pairs={{0,3},{1,0},{2,1},{3,2},{4,7},{5,4},{6,5},{7,6},{8,11},{9,8},{10,9... | collective-permute-start | bytes 102152 | tf_op jit(solution)/shard_map/ppermute | solution.py:535
  6.7 4.4 %collective-permute-start.3 = (f32[40,128]{1,0:T(8,128)}, f32[40,128]{1,0:T(8,128)}, u32[]{:S(2)}, u32[]{:S(2)}) collective-permute-start(f32[40,128]{1,0:T(8,128)} %get-tuple-element.16), channel_id=1, source_target_pairs={{3,4},{7,8},{11,12},{15,16},{19,20},{23,24},{27,28},{31,32},{35,36... | collective-permute-start | bytes 61448 | tf_op jit(solution)/shard_map/ppermute | solution.py:537
  11.1 0.1 collective-permute-start.1
  11.2 4.4 %collective-permute-done.1.c2 = f32[16,152]{1,0:T(8,128)} collective-permute-done((f32[16,152]{1,0:T(8,128)}, f32[16,152]{1,0:T(8,128)}, u32[]{:S(2)}, u32[]{:S(2)}) %collective-permute-start.1) | collective-permute-done | bytes 9760 | tf_op jit(solution)/shard_map/ppermute | solution.py:535
  15.6 0.0 collective-permute-done.3.cross
  15.6 0.0 collective-permute-done.x1
  15.6 0.0 collective-permute-done.2.x3
  15.6 2.4 %pack.1 = bf16[4096,128]{1,0:T(8,128)(2,1)} custom-call(s32[2,128]{1,0:T(2,128)} %bitcast.15, s32[1,128]{1,0:T(1,128)} %counts.1, bf16[64,152]{1,0:T(8,128)(2,1)} %get-tuple-element.11.mult, f32[16,152]{1,0:T(8,128)} %get-tuple-element.12.c0, f32[56,152]{1,0:T(8,128)} %collective-permute-done.x1, f32[16,152]{1,0:T(8,128)} %collective-permute-done.1.c2, ...), custom_call_target="tpu_custom_call" | custom-call | tf_op jit(solution)/shard_map/pack/pallas_call | solution.py:142
  18.0 9.9 %all-to-all-start = ((bf16[128,32,128]{2,1,0:T(8,128)(2,1)}), bf16[128,32,128]{2,1,0:T(8,128)(2,1)}, u32[]{:S(2)}, u32[]{:S(2)}) async-start(bf16[128,32,128]{2,1,0:T(8,128)(2,1)} %bitcast.11), calls=%async_computation | async-start | bytes 2097152 | tf_op jit(solution)/shard_map/all_to_all | solution.py:540
  28.0 14.2 %near.1.near_part = f32[64,128]{1,0:T(8,128)} custom-call(s32[16,27]{1,0:T(8,128)} %index.1, s32[16]{0:T(128)} %count.1, f32[3,16,128]{2,1,0:T(8,128)} %cen.3, f32[3,16,128]{2,1,0:T(8,128)} %nrm.3, f32[64,128]{1,0:T(8,128)} %bitcast.14, f32[56,152]{1,0:T(8,128)} %collective-permute-done.x1, f32[56,152]{1,0:T(8,128)} %collective-permute-done.2.x3, ...), custom_call_target="tpu_custom_call" | custom-call | flops 2000000000 | bytes 1000000 | tf_op jit(solution)/shard_map/near/pallas_call | solution.py:270
  42.1 5.1 %all-to-all-done = bf16[128,32,128]{2,1,0:T(8,128)(2,1)} async-done(((bf16[128,32,128]{2,1,0:T(8,128)(2,1)}), bf16[128,32,128]{2,1,0:T(8,128)(2,1)}, u32[]{:S(2)}, u32[]{:S(2)}) %all-to-all-start) | async-done | bytes 1048608 | tf_op jit(solution)/shard_map/all_to_all | solution.py:540
  47.2 24.0 %finish.1 = f32[64,128]{1,0:T(8,128)} custom-call(s32[1,16]{1,0:T(1,128)} %par.3, s32[1,16]{1,0:T(1,128)} %octs.3, s32[16]{0:T(128)} %far_count.1, s32[16]{0:T(128)} %top_count.1, s32[16,64]{1,0:T(8,128)} %far_slot.1, s32[16,64]{1,0:T(8,128)} %far_op.1, s32[16,32]{1,0:T(8,128)} %top_src.1, s32[16,32]{1,0:T(8,128)} %top_op.1, ...), custom_call_target="tpu_custom_call" | custom-call | tf_op jit(solution)/shard_map/finish/pallas_call | solution.py:458
Async XLA Ops:
  3.3 12.3 %collective-permute-start = (f32[56,152]{1,0:T(8,128)}, f32[56,152]{1,0:T(8,128)}, u32[]{:S(2)}, u32[]{:S(2)}) collective-permute-start(f32[56,152]{1,0:T(8,128)} %get-tuple-element.13), channel_id=1, source_target_pairs={{0,1},{1,2},{2,3},{3,0},{4,5},{5,6},{6,7},{7,4},{8,9},{9,10},{10,1... | collective-permute-start | bytes 102152 | tf_op jit(solution)/shard_map/ppermute | solution.py:535
  5.3 10.3 %collective-permute-start.2 = (f32[56,152]{1,0:T(8,128)}, f32[56,152]{1,0:T(8,128)}, u32[]{:S(2)}, u32[]{:S(2)}) collective-permute-start(f32[56,152]{1,0:T(8,128)} %get-tuple-element.15), channel_id=1, source_target_pairs={{0,3},{1,0},{2,1},{3,2},{4,7},{5,4},{6,5},{7,6},{8,11},{9,8},{10,9... | collective-permute-start | bytes 102152 | tf_op jit(solution)/shard_map/ppermute | solution.py:535
  6.7 8.9 %collective-permute-start.3 = (f32[40,128]{1,0:T(8,128)}, f32[40,128]{1,0:T(8,128)}, u32[]{:S(2)}, u32[]{:S(2)}) collective-permute-start(f32[40,128]{1,0:T(8,128)} %get-tuple-element.16), channel_id=1, source_target_pairs={{3,4},{7,8},{11,12},{15,16},{19,20},{23,24},{27,28},{31,32},{35,36... | collective-permute-start | bytes 61448 | tf_op jit(solution)/shard_map/ppermute | solution.py:537
  11.1 4.5 %collective-permute-start.1 = (f32[16,152]{1,0:T(8,128)}, f32[16,152]{1,0:T(8,128)}, u32[]{:S(2)}, u32[]{:S(2)}) collective-permute-start(f32[16,152]{1,0:T(8,128)} %get-tuple-element.14), channel_id=1, source_target_pairs={{0,2},{1,3},{2,0},{3,1},{4,6},{5,7},{6,4},{7,5},{8,10},{9,11},{10,... | collective-permute-start | bytes 29192 | tf_op jit(solution)/shard_map/ppermute | solution.py:535
  18.0 29.2 %all-to-all-start = ((bf16[128,32,128]{2,1,0:T(8,128)(2,1)}), bf16[128,32,128]{2,1,0:T(8,128)(2,1)}, u32[]{:S(2)}, u32[]{:S(2)}) async-start(bf16[128,32,128]{2,1,0:T(8,128)(2,1)} %bitcast.11), calls=%async_computation | async-start | bytes 2097152 | tf_op jit(solution)/shard_map/all_to_all | solution.py:540

commit v5 on v4

--- a/solution.py
+++ b/solution.py
@@ -103,53 +103,84 @@
     )(par, octs, dens, cen, nrm, tm, m2m)
 
 
-def pack_kernel(boxes, counts, mult, c0, x1, c2, x3, cross, out, far, const):
+def boxes_of(mats):
     row = iota((EQ, BOX), 0)
     lane = iota((EQ, BOX), 1)
-    own = (c0[...] + x1[:16, :]) + (c2[...] + x3[:16, :])
-    own = own.astype(bf16).astype(f32)
+    table = jnp.zeros((mats[0].shape[0], BOX), f32)
+    for r, mat in enumerate(mats):
+        place = (lane == row + EQ * r).astype(f32).astype(bf16)
+        table = table + nn(mat, place)
+    return table
+
+
+def choose_kernel(boxes, counts, mult, out, far):
     mf = mult[...].astype(f32)
-    table = jnp.zeros((24, BOX), f32)
-    for r in range(RHS):
-        both = jnp.concatenate(
-            [mf[16 * r : 16 * r + 16], own[4 * r : 4 * r + 4], jnp.zeros((4, EQ), f32)], 0
-        )
-        place = (lane == row + EQ * r).astype(f32).astype(bf16)
-        table = table + nn(both.astype(bf16), place)
+    table = boxes_of([mf[LEAF * r : LEAF * (r + 1)].astype(bf16) for r in range(RHS)]).astype(bf16)
     leaf = iota((LEAF, PAN), 0)
     for j in range(2):
         hot = ((boxes[j : j + 1, :] == leaf) & (counts[...] > j)).astype(f32).T
-        y = nn(hot.astype(bf16), table[:LEAF].astype(bf16))
+        y = nn(hot.astype(bf16), table)
         for t in range(PIECES):
             far[pl.ds(PIECES * j + t, PAN, stride=24), :] = y[:, PAN * t : PAN * (t + 1)]
-    const[...] = jnp.zeros_like(const)
-    for q in range(4):
-        for t in range(PIECES):
-            at = PIECES * (2 + q) + t
-            const[at : at + 1, :] = table[LEAF + q : LEAF + q + 1, PAN * t : PAN * (t + 1)]
+    is_far = iota((16, PAN), 0) < 2 * PIECES
+    for d in range(PAN):
+        out[16 * d : 16 * (d + 1), :] = jnp.where(is_far, far[24 * d : 24 * d + 16, :], 0.0).astype(
+            bf16
+        )
+
+
+def choose(boxes, counts, mult):
+    outs = jax.ShapeDtypeStruct((PAN * 16, PAN), bf16)
+    return pl.pallas_call(
+        choose_kernel,
+        grid=(1,),
+        in_specs=[whole(x) for x in (boxes, counts, mult)],
+        out_specs=whole(outs),
+        out_shape=outs,
+        scratch_shapes=[pltpu.VMEM((PAN * 24, PAN), f32)],
+        compiler_params=pltpu.CompilerParams(vmem_limit_bytes=BIG),
+        name="choose",
+    )(boxes, counts, mult)
+
+
+def pack_kernel(far, c0, x1, c2, x3, cross, out, const):
+    @pl.when(pl.program_id(0) == 0)
+    def _():
+        own = (c0[...] + x1[:16, :]) + (c2[...] + x3[:16, :])
+        own = own.astype(bf16).astype(f32)
+        pad = jnp.zeros((4, EQ), f32)
+        table = boxes_of(
+            [jnp.concatenate([own[4 * r : 4 * r + 4], pad], 0).astype(bf16) for r in range(RHS)]
+        )
+        const[...] = jnp.zeros_like(const)
+        for q in range(4):
+            for t in range(PIECES):
+                at = PIECES * (2 + q) + t
+                const[at : at + 1, :] = table[q : q + 1, PAN * t : PAN * (t + 1)]
+
     head = const[:16]
     rest = const[16:].astype(bf16)
-    is_far = iota((16, PAN), 0) < 2 * PIECES
-    for d in range(PAN):
-        out[CHUNK * d : CHUNK * d + 16, :] = jnp.where(
-            is_far, far[24 * d : 24 * d + 16, :], head
+    for d in range(far.shape[0] // 16):
+        out[CHUNK * d : CHUNK * d + 16, :] = (
+            far[16 * d : 16 * (d + 1), :].astype(f32) + head
         ).astype(bf16)
         out[CHUNK * d + 16 : CHUNK * (d + 1), :] = rest
 
 
-def pack(boxes, counts, mult, pieces, later):
-    outs = jax.ShapeDtypeStruct((PAN * CHUNK, PAN), bf16)
+def pack(far, pieces, later):
+    steps = 2
     return pl.pallas_call(
         pack_kernel,
-        grid=(1,),
-        in_specs=[whole(x) for x in (boxes, counts, mult, *pieces)]
+        grid=(steps,),
+        in_specs=[pl.BlockSpec((PAN * 16 // steps, PAN), lambda i: (i, 0))]
+        + [whole(x) for x in pieces]
         + [pl.BlockSpec(memory_space=pl.ANY)] * len(later),
-        out_specs=whole(outs),
-        out_shape=outs,
-        scratch_shapes=[pltpu.VMEM((PAN * 24, PAN), f32), pltpu.VMEM((CHUNK, PAN), f32)],
+        out_specs=pl.BlockSpec((PAN * CHUNK // steps, PAN), lambda i: (i, 0)),
+        out_shape=jax.ShapeDtypeStruct((PAN * CHUNK, PAN), bf16),
+        scratch_shapes=[pltpu.VMEM((CHUNK, PAN), f32)],
         compiler_params=pltpu.CompilerParams(vmem_limit_bytes=BIG),
         name="pack",
-    )(boxes, counts, mult, *pieces, *later)
+    )(far, *pieces, *later)
 
 
 SRC = LEAF + 2 * RIM
@@ -536,7 +567,8 @@
     ends = range(subs - 1, count - 1, subs)
     cross = lax.ppermute(cross, axes, [(i, i + 1) for i in ends] + [(i + 1, i) for i in ends])
 
-    outgoing = pack(jnp.transpose(send_box[0]), send_count, mult, pieces, (cross,))
+    chosen = choose(jnp.transpose(send_box[0]), send_count, mult)
+    outgoing = pack(chosen, pieces, (cross,))
     arrived = lax.all_to_all(
         outgoing.reshape(count, CHUNK, PAN), axes, split_axis=0, concat_axis=0, tiled=True
     )

time: 71.7 us -> 71.7 us (level)
    ppermute x3, waiting for transfers between devices: 4.4 us -> 2.33 us  [per_device(): lax.ppermute(piece, 'sub', [(i, (i + s) % subs) for i in range(subs)])]
    pallas_call x1 -> x2, Pallas kernels: 2.41 us -> 4.26 us  [the longest x1 2.2 us: pack(): pl.pallas_call(pack_kernel, grid=(steps,), in_specs=[pl.BlockSpec((PAN *...]
    all_to_all x1, waiting for transfers between devices: 5.05 us -> 6.46 us  [per_device(): lax.all_to_all(outgoing.reshape(count, CHUNK, PAN), axes, split_axis=0, c...]
    pallas_call x1, Pallas kernels: 14.2 us -> 12.8 us  [near(): pl.pallas_call(near_kernel, grid=(1,), in_specs=[SM, SM] + [whole(x) for...]
  transfers between devices with their start and end apart: 5 -> 5, of which waited for: 2 -> 2; matrix products, arithmetic and copies ran while one was open for 0% -> 0% of each run, Pallas kernels for 20% -> 21%
where the time goes in v5:
time: 71.7 us; the launch traced here: 71.2 us
  Pallas kernels  44.3 us (62%)
  starting transfers between devices  17.8 us (25%)
  waiting for transfers between devices  8.8 us (12%)
    pallas_call x1, Pallas kernels, finish(): pl.pallas_call(finish_kernel, grid=(chunks + 1,), in_specs=[SM, SM, SM, S...  24 us
    pallas_call x1, Pallas kernels, near(): pl.pallas_call(near_kernel, grid=(1,), in_specs=[SM, SM] + [whole(x) for...  12.8 us
    all_to_all x1, starting transfers between devices, per_device(): lax.all_to_all(outgoing.reshape(count, CHUNK, PAN), axes, split_axis=0, c...  9.96 us
    all_to_all x1, waiting for transfers between devices, per_device(): lax.all_to_all(outgoing.reshape(count, CHUNK, PAN), axes, split_axis=0, c...  6.46 us
    ppermute x1, starting transfers between devices, per_device(): lax.ppermute(cross, axes, [(i, i + 1) for i in ends] + [(i + 1, i) for i...  4.42 us
    ppermute x3, starting transfers between devices, per_device(): lax.ppermute(piece, 'sub', [(i, (i + s) % subs) for i in range(subs)])  3.47 us
    pallas_call x1, Pallas kernels, upward(): pl.pallas_call(upward_kernel, grid=(1,), in_specs=[SM, SM] + [whole(x) fo...  3.28 us
    ppermute x3, waiting for transfers between devices, per_device(): lax.ppermute(piece, 'sub', [(i, (i + s) % subs) for i in range(subs)])  2.33 us
  transfers between devices with their start and end apart: 5, of which 2 were waited for; matrix products, arithmetic and copies ran while one was open for 0% of the time, Pallas kernels for 21%

profile of v5, /device:TPU:1, one launch (start us, length us, event | category | flops | bytes accessed | tf_op | source)
XLA Modules:
  0.0 71.2 jit_solution(18241490590021673355)
XLA Ops:
  0.0 3.3 %upward.1 = (bf16[64,152]{1,0:T(8,128)(2,1)}, f32[16,152]{1,0:T(8,128)}, f32[56,152]{1,0:T(8,128)}, f32[16,152]{1,0:T(8,128)}, f32[56,152]{1,0:T(8,128)}, /*index=5*/f32[40,128]{1,0:T(8,128)}) custom-call(s32[1,16]{1,0:T(1,128)} %par.3, s32[1,16]{1,0:T(1,128)} %octs.3, f32[64,128]{1,0:T(8,128)} %bitcast.13, f32[3,16,128]{2,1,0:T(8,128)} %cen.3, ...), custom_call_target="tpu_custom_call" | custom-call | tf_op jit(solution)/shard_map/upward/pallas_call | solution.py:95
  3.3 2.1 %collective-permute-start = (f32[56,152]{1,0:T(8,128)}, f32[56,152]{1,0:T(8,128)}, u32[]{:S(2)}, u32[]{:S(2)}) collective-permute-start(f32[56,152]{1,0:T(8,128)} %get-tuple-element.13), channel_id=1, source_target_pairs={{0,1},{1,2},{2,3},{3,0},{4,5},{5,6},{6,7},{7,4},{8,9},{9,10},{10,1... | collective-permute-start | bytes 102152 | tf_op jit(solution)/shard_map/ppermute | solution.py:566
  5.3 1.3 %collective-permute-start.2 = (f32[56,152]{1,0:T(8,128)}, f32[56,152]{1,0:T(8,128)}, u32[]{:S(2)}, u32[]{:S(2)}) collective-permute-start(f32[56,152]{1,0:T(8,128)} %get-tuple-element.15), channel_id=1, source_target_pairs={{0,3},{1,0},{2,1},{3,2},{4,7},{5,4},{6,5},{7,6},{8,11},{9,8},{10,9... | collective-permute-start | bytes 102152 | tf_op jit(solution)/shard_map/ppermute | solution.py:566
  6.7 4.4 %collective-permute-start.3 = (f32[40,128]{1,0:T(8,128)}, f32[40,128]{1,0:T(8,128)}, u32[]{:S(2)}, u32[]{:S(2)}) collective-permute-start(f32[40,128]{1,0:T(8,128)} %get-tuple-element.16), channel_id=1, source_target_pairs={{3,4},{7,8},{11,12},{15,16},{19,20},{23,24},{27,28},{31,32},{35,36... | collective-permute-start | bytes 61448 | tf_op jit(solution)/shard_map/ppermute | solution.py:568
  11.1 0.1 collective-permute-start.1
  11.2 2.1 %choose.1.far = bf16[2048,128]{1,0:T(8,128)(2,1)} custom-call(s32[2,128]{1,0:T(2,128)} %bitcast.15, s32[1,128]{1,0:T(1,128)} %counts.1, bf16[64,152]{1,0:T(8,128)(2,1)} %get-tuple-element.11.mult), custom_call_target="tpu_custom_call" | custom-call | tf_op jit(solution)/shard_map/choose/pallas_call | solution.py:134
  13.2 2.3 %collective-permute-done.1.c2 = f32[16,152]{1,0:T(8,128)} collective-permute-done((f32[16,152]{1,0:T(8,128)}, f32[16,152]{1,0:T(8,128)}, u32[]{:S(2)}, u32[]{:S(2)}) %collective-permute-start.1) | collective-permute-done | bytes 9760 | tf_op jit(solution)/shard_map/ppermute | solution.py:566
  15.6 0.0 collective-permute-done.3.cross
  15.6 0.0 collective-permute-done.x1
  15.6 0.0 collective-permute-done.2.x3
  15.6 2.2 %pack.1 = bf16[4096,128]{1,0:T(8,128)(2,1)} custom-call(bf16[2048,128]{1,0:T(8,128)(2,1)} %choose.1.far, f32[16,152]{1,0:T(8,128)} %get-tuple-element.12.c0, f32[56,152]{1,0:T(8,128)} %collective-permute-done.x1, f32[16,152]{1,0:T(8,128)} %collective-permute-done.1.c2, f32[56,152]{1,0:T(8,128)} %collective-permute-done.2.x3, ...), custom_call_target="tpu_custom_call" | custom-call | tf_op jit(solution)/shard_map/pack/pallas_call | solution.py:172
  17.8 10.0 %all-to-all-start = ((bf16[128,32,128]{2,1,0:T(8,128)(2,1)}), bf16[128,32,128]{2,1,0:T(8,128)(2,1)}, u32[]{:S(2)}, u32[]{:S(2)}) async-start(bf16[128,32,128]{2,1,0:T(8,128)(2,1)} %bitcast.11), calls=%async_computation | async-start | bytes 2097152 | tf_op jit(solution)/shard_map/all_to_all | solution.py:572
  27.7 12.8 %near.1.near_part = f32[64,128]{1,0:T(8,128)} custom-call(s32[16,27]{1,0:T(8,128)} %index.1, s32[16]{0:T(128)} %count.1, f32[3,16,128]{2,1,0:T(8,128)} %cen.3, f32[3,16,128]{2,1,0:T(8,128)} %nrm.3, f32[64,128]{1,0:T(8,128)} %bitcast.14, f32[56,152]{1,0:T(8,128)} %collective-permute-done.x1, f32[56,152]{1,0:T(8,128)} %collective-permute-done.2.x3, ...), custom_call_target="tpu_custom_call" | custom-call | flops 2000000000 | bytes 1000000 | tf_op jit(solution)/shard_map/near/pallas_call | solution.py:301
  40.5 6.5 %all-to-all-done = bf16[128,32,128]{2,1,0:T(8,128)(2,1)} async-done(((bf16[128,32,128]{2,1,0:T(8,128)(2,1)}), bf16[128,32,128]{2,1,0:T(8,128)(2,1)}, u32[]{:S(2)}, u32[]{:S(2)}) %all-to-all-start) | async-done | bytes 1048608 | tf_op jit(solution)/shard_map/all_to_all | solution.py:572
  47.0 24.0 %finish.1 = f32[64,128]{1,0:T(8,128)} custom-call(s32[1,16]{1,0:T(1,128)} %par.3, s32[1,16]{1,0:T(1,128)} %octs.3, s32[16]{0:T(128)} %far_count.1, s32[16]{0:T(128)} %top_count.1, s32[16,64]{1,0:T(8,128)} %far_slot.1, s32[16,64]{1,0:T(8,128)} %far_op.1, s32[16,32]{1,0:T(8,128)} %top_src.1, s32[16,32]{1,0:T(8,128)} %top_op.1, ...), custom_call_target="tpu_custom_call" | custom-call | tf_op jit(solution)/shard_map/finish/pallas_call | solution.py:489
Async XLA Ops:
  3.3 12.3 %collective-permute-start = (f32[56,152]{1,0:T(8,128)}, f32[56,152]{1,0:T(8,128)}, u32[]{:S(2)}, u32[]{:S(2)}) collective-permute-start(f32[56,152]{1,0:T(8,128)} %get-tuple-element.13), channel_id=1, source_target_pairs={{0,1},{1,2},{2,3},{3,0},{4,5},{5,6},{6,7},{7,4},{8,9},{9,10},{10,1... | collective-permute-start | bytes 102152 | tf_op jit(solution)/shard_map/ppermute | solution.py:566
  5.3 10.3 %collective-permute-start.2 = (f32[56,152]{1,0:T(8,128)}, f32[56,152]{1,0:T(8,128)}, u32[]{:S(2)}, u32[]{:S(2)}) collective-permute-start(f32[56,152]{1,0:T(8,128)} %get-tuple-element.15), channel_id=1, source_target_pairs={{0,3},{1,0},{2,1},{3,2},{4,7},{5,4},{6,5},{7,6},{8,11},{9,8},{10,9... | collective-permute-start | bytes 102152 | tf_op jit(solution)/shard_map/ppermute | solution.py:566
  6.7 8.9 %collective-permute-start.3 = (f32[40,128]{1,0:T(8,128)}, f32[40,128]{1,0:T(8,128)}, u32[]{:S(2)}, u32[]{:S(2)}) collective-permute-start(f32[40,128]{1,0:T(8,128)} %get-tuple-element.16), channel_id=1, source_target_pairs={{3,4},{7,8},{11,12},{15,16},{19,20},{23,24},{27,28},{31,32},{35,36... | collective-permute-start | bytes 61448 | tf_op jit(solution)/shard_map/ppermute | solution.py:568
  11.1 4.5 %collective-permute-start.1 = (f32[16,152]{1,0:T(8,128)}, f32[16,152]{1,0:T(8,128)}, u32[]{:S(2)}, u32[]{:S(2)}) collective-permute-start(f32[16,152]{1,0:T(8,128)} %get-tuple-element.14), channel_id=1, source_target_pairs={{0,2},{1,3},{2,0},{3,1},{4,6},{5,7},{6,4},{7,5},{8,10},{9,11},{10,... | collective-permute-start | bytes 29192 | tf_op jit(solution)/shard_map/ppermute | solution.py:566
  17.8 29.2 %all-to-all-start = ((bf16[128,32,128]{2,1,0:T(8,128)(2,1)}), bf16[128,32,128]{2,1,0:T(8,128)(2,1)}, u32[]{:S(2)}, u32[]{:S(2)}) async-start(bf16[128,32,128]{2,1,0:T(8,128)(2,1)} %bitcast.11), calls=%async_computation | async-start | bytes 2097152 | tf_op jit(solution)/shard_map/all_to_all | solution.py:572

commit v6 on v4

--- a/solution.py
+++ b/solution.py
@@ -153,7 +153,7 @@
 
 
 SRC = LEAF + 2 * RIM
-BATCH = 4
+BATCH = 3
 FEAT = 48
 ORDERS = ((0, 0), (0, 1), (1, 0), (0, 2), (1, 1), (2, 0))
 

time: 71.7 us -> 71.7 us (level)
  Pallas kernels: 43.9 us -> 42.9 us
  waiting for transfers between devices: 9.46 us -> 10.4 us
    pallas_call x1, Pallas kernels: 14.2 us -> 13.2 us  [near(): pl.pallas_call(near_kernel, grid=(1,), in_specs=[SM, SM] + [whole(x) for...]
    all_to_all x1, waiting for transfers between devices: 5.05 us -> 6.03 us  [per_device(): lax.all_to_all(outgoing.reshape(count, CHUNK, PAN), axes, split_axis=0, c...]
  transfers between devices with their start and end apart: 5 -> 5, of which waited for: 2 -> 2; matrix products, arithmetic and copies ran while one was open for 0% -> 0% of each run, Pallas kernels for 20% -> 19%
where the time goes in v6:
time: 71.7 us; the launch traced here: 71.2 us
  Pallas kernels  42.9 us (60%)
  starting transfers between devices  17.8 us (25%)
  waiting for transfers between devices  10.4 us (15%)
    pallas_call x1, Pallas kernels, finish(): pl.pallas_call(finish_kernel, grid=(chunks + 1,), in_specs=[SM, SM, SM, S...  24 us
    pallas_call x1, Pallas kernels, near(): pl.pallas_call(near_kernel, grid=(1,), in_specs=[SM, SM] + [whole(x) for...  13.2 us
    all_to_all x1, starting transfers between devices, per_device(): lax.all_to_all(outgoing.reshape(count, CHUNK, PAN), axes, split_axis=0, c...  9.95 us
    all_to_all x1, waiting for transfers between devices, per_device(): lax.all_to_all(outgoing.reshape(count, CHUNK, PAN), axes, split_axis=0, c...  6.03 us
    ppermute x1, starting transfers between devices, per_device(): lax.ppermute(cross, axes, [(i, i + 1) for i in ends] + [(i + 1, i) for i...  4.41 us
    ppermute x3, waiting for transfers between devices, per_device(): lax.ppermute(piece, 'sub', [(i, (i + s) % subs) for i in range(subs)])  4.4 us
    ppermute x3, starting transfers between devices, per_device(): lax.ppermute(piece, 'sub', [(i, (i + s) % subs) for i in range(subs)])  3.46 us
    pallas_call x1, Pallas kernels, upward(): pl.pallas_call(upward_kernel, grid=(1,), in_specs=[SM, SM] + [whole(x) fo...  3.29 us
  transfers between devices with their start and end apart: 5, of which 2 were waited for; matrix products, arithmetic and copies ran while one was open for 0% of the time, Pallas kernels for 19%

profile of v6, /device:TPU:1, one launch (start us, length us, event | category | flops | bytes accessed | tf_op | source)
XLA Modules:
  0.0 71.2 jit_solution(5185453139706415292)
XLA Ops:
  0.0 3.3 %upward.1 = (bf16[64,152]{1,0:T(8,128)(2,1)}, f32[16,152]{1,0:T(8,128)}, f32[56,152]{1,0:T(8,128)}, f32[16,152]{1,0:T(8,128)}, f32[56,152]{1,0:T(8,128)}, /*index=5*/f32[40,128]{1,0:T(8,128)}) custom-call(s32[1,16]{1,0:T(1,128)} %par.3, s32[1,16]{1,0:T(1,128)} %octs.3, f32[64,128]{1,0:T(8,128)} %bitcast.13, f32[3,16,128]{2,1,0:T(8,128)} %cen.3, ...), custom_call_target="tpu_custom_call" | custom-call | tf_op jit(solution)/shard_map/upward/pallas_call | solution.py:95
  3.3 2.0 %collective-permute-start = (f32[56,152]{1,0:T(8,128)}, f32[56,152]{1,0:T(8,128)}, u32[]{:S(2)}, u32[]{:S(2)}) collective-permute-start(f32[56,152]{1,0:T(8,128)} %get-tuple-element.13), channel_id=1, source_target_pairs={{0,1},{1,2},{2,3},{3,0},{4,5},{5,6},{6,7},{7,4},{8,9},{9,10},{10,1... | collective-permute-start | bytes 102152 | tf_op jit(solution)/shard_map/ppermute | solution.py:535
  5.3 1.3 %collective-permute-start.2 = (f32[56,152]{1,0:T(8,128)}, f32[56,152]{1,0:T(8,128)}, u32[]{:S(2)}, u32[]{:S(2)}) collective-permute-start(f32[56,152]{1,0:T(8,128)} %get-tuple-element.15), channel_id=1, source_target_pairs={{0,3},{1,0},{2,1},{3,2},{4,7},{5,4},{6,5},{7,6},{8,11},{9,8},{10,9... | collective-permute-start | bytes 102152 | tf_op jit(solution)/shard_map/ppermute | solution.py:535
  6.7 4.4 %collective-permute-start.3 = (f32[40,128]{1,0:T(8,128)}, f32[40,128]{1,0:T(8,128)}, u32[]{:S(2)}, u32[]{:S(2)}) collective-permute-start(f32[40,128]{1,0:T(8,128)} %get-tuple-element.16), channel_id=1, source_target_pairs={{3,4},{7,8},{11,12},{15,16},{19,20},{23,24},{27,28},{31,32},{35,36... | collective-permute-start | bytes 61448 | tf_op jit(solution)/shard_map/ppermute | solution.py:537
  11.1 0.1 collective-permute-start.1
  11.2 4.4 %collective-permute-done.1.c2 = f32[16,152]{1,0:T(8,128)} collective-permute-done((f32[16,152]{1,0:T(8,128)}, f32[16,152]{1,0:T(8,128)}, u32[]{:S(2)}, u32[]{:S(2)}) %collective-permute-start.1) | collective-permute-done | bytes 9760 | tf_op jit(solution)/shard_map/ppermute | solution.py:535
  15.6 0.0 collective-permute-done.3.cross
  15.6 0.0 collective-permute-done.x1
  15.6 0.0 collective-permute-done.2.x3
  15.6 2.4 %pack.1 = bf16[4096,128]{1,0:T(8,128)(2,1)} custom-call(s32[2,128]{1,0:T(2,128)} %bitcast.15, s32[1,128]{1,0:T(1,128)} %counts.1, bf16[64,152]{1,0:T(8,128)(2,1)} %get-tuple-element.11.mult, f32[16,152]{1,0:T(8,128)} %get-tuple-element.12.c0, f32[56,152]{1,0:T(8,128)} %collective-permute-done.x1, f32[16,152]{1,0:T(8,128)} %collective-permute-done.1.c2, ...), custom_call_target="tpu_custom_call" | custom-call | tf_op jit(solution)/shard_map/pack/pallas_call | solution.py:142
  18.0 9.9 %all-to-all-start = ((bf16[128,32,128]{2,1,0:T(8,128)(2,1)}), bf16[128,32,128]{2,1,0:T(8,128)(2,1)}, u32[]{:S(2)}, u32[]{:S(2)}) async-start(bf16[128,32,128]{2,1,0:T(8,128)(2,1)} %bitcast.11), calls=%async_computation | async-start | bytes 2097152 | tf_op jit(solution)/shard_map/all_to_all | solution.py:540
  28.0 13.2 %near.1.near_part = f32[64,128]{1,0:T(8,128)} custom-call(s32[16,27]{1,0:T(8,128)} %index.1, s32[16]{0:T(128)} %count.1, f32[3,16,128]{2,1,0:T(8,128)} %cen.3, f32[3,16,128]{2,1,0:T(8,128)} %nrm.3, f32[64,128]{1,0:T(8,128)} %bitcast.14, f32[56,152]{1,0:T(8,128)} %collective-permute-done.x1, f32[56,152]{1,0:T(8,128)} %collective-permute-done.2.x3, ...), custom_call_target="tpu_custom_call" | custom-call | flops 2000000000 | bytes 1000000 | tf_op jit(solution)/shard_map/near/pallas_call | solution.py:270
  41.2 6.0 %all-to-all-done = bf16[128,32,128]{2,1,0:T(8,128)(2,1)} async-done(((bf16[128,32,128]{2,1,0:T(8,128)(2,1)}), bf16[128,32,128]{2,1,0:T(8,128)(2,1)}, u32[]{:S(2)}, u32[]{:S(2)}) %all-to-all-start) | async-done | bytes 1048608 | tf_op jit(solution)/shard_map/all_to_all | solution.py:540
  47.2 24.0 %finish.1 = f32[64,128]{1,0:T(8,128)} custom-call(s32[1,16]{1,0:T(1,128)} %par.3, s32[1,16]{1,0:T(1,128)} %octs.3, s32[16]{0:T(128)} %far_count.1, s32[16]{0:T(128)} %top_count.1, s32[16,64]{1,0:T(8,128)} %far_slot.1, s32[16,64]{1,0:T(8,128)} %far_op.1, s32[16,32]{1,0:T(8,128)} %top_src.1, s32[16,32]{1,0:T(8,128)} %top_op.1, ...), custom_call_target="tpu_custom_call" | custom-call | tf_op jit(solution)/shard_map/finish/pallas_call | solution.py:458
Async XLA Ops:
  3.3 12.3 %collective-permute-start = (f32[56,152]{1,0:T(8,128)}, f32[56,152]{1,0:T(8,128)}, u32[]{:S(2)}, u32[]{:S(2)}) collective-permute-start(f32[56,152]{1,0:T(8,128)} %get-tuple-element.13), channel_id=1, source_target_pairs={{0,1},{1,2},{2,3},{3,0},{4,5},{5,6},{6,7},{7,4},{8,9},{9,10},{10,1... | collective-permute-start | bytes 102152 | tf_op jit(solution)/shard_map/ppermute | solution.py:535
  5.3 10.3 %collective-permute-start.2 = (f32[56,152]{1,0:T(8,128)}, f32[56,152]{1,0:T(8,128)}, u32[]{:S(2)}, u32[]{:S(2)}) collective-permute-start(f32[56,152]{1,0:T(8,128)} %get-tuple-element.15), channel_id=1, source_target_pairs={{0,3},{1,0},{2,1},{3,2},{4,7},{5,4},{6,5},{7,6},{8,11},{9,8},{10,9... | collective-permute-start | bytes 102152 | tf_op jit(solution)/shard_map/ppermute | solution.py:535
  6.7 8.9 %collective-permute-start.3 = (f32[40,128]{1,0:T(8,128)}, f32[40,128]{1,0:T(8,128)}, u32[]{:S(2)}, u32[]{:S(2)}) collective-permute-start(f32[40,128]{1,0:T(8,128)} %get-tuple-element.16), channel_id=1, source_target_pairs={{3,4},{7,8},{11,12},{15,16},{19,20},{23,24},{27,28},{31,32},{35,36... | collective-permute-start | bytes 61448 | tf_op jit(solution)/shard_map/ppermute | solution.py:537
  11.1 4.5 %collective-permute-start.1 = (f32[16,152]{1,0:T(8,128)}, f32[16,152]{1,0:T(8,128)}, u32[]{:S(2)}, u32[]{:S(2)}) collective-permute-start(f32[16,152]{1,0:T(8,128)} %get-tuple-element.14), channel_id=1, source_target_pairs={{0,2},{1,3},{2,0},{3,1},{4,6},{5,7},{6,4},{7,5},{8,10},{9,11},{10,... | collective-permute-start | bytes 29192 | tf_op jit(solution)/shard_map/ppermute | solution.py:535
  18.0 29.2 %all-to-all-start = ((bf16[128,32,128]{2,1,0:T(8,128)(2,1)}), bf16[128,32,128]{2,1,0:T(8,128)(2,1)}, u32[]{:S(2)}, u32[]{:S(2)}) async-start(bf16[128,32,128]{2,1,0:T(8,128)(2,1)} %bitcast.11), calls=%async_computation | async-start | bytes 2097152 | tf_op jit(solution)/shard_map/all_to_all | solution.py:540
